TPU v7x, 512 devices: a whole 4x4x16 slice. The times are simulated.
512 devices in a mesh: lat: 64 (over y, z), lon: 8 (over x, core).
Axes of the slice: x: 4, y: 4, z: 16, core: 2. Of those that a mesh axis runs over, the one named last changes fastest.
Arguments:
- covariance: float32 [64, 64, 128, 128], P('lat', None, 'lon'), may hold values from -6 to 6
- winds: float32 [2, 3, 64, 128], P(None, None, None, 'lon'), may hold values from -0.35 to 0.35
- diffusivity: float32 [64, 128], P(None, 'lon'), may hold values from 0.01 to 0.07
- cutoff: int32 [64], replicated, may hold values from 4 to 16, as said below
Outputs:
- forecast: float32 [64, 64, 128, 128], P('lat', None, 'lon')
Inputs may be any that keep to these rules, and one draw needn't show every extreme that they name: Some latitude has cutoff 16 and some other has 4.
All inputs are finite; a program needn't handle non-finite values.
Results may differ from a plain program's by a relative error of at most 0.00002.
Values sent between devices are 32-bit elements; how exact they have to be, the bound alone decides.
A program may use at most 192 MiB of HBM per device.

v0:
```python
import jax
import jax.numpy as jnp
from jax import lax
from jax.sharding import PartitionSpec as P

STEPS = 3


def extended_2(block, sides, width):
    for axis, dim in sides:
        count = lax.axis_size(axis)
        forward = [(i, i + 1) for i in range(count - 1)]
        forward.append((count - 1, 0))
        backward = [(target, source) for source, target in forward]
        low = lax.ppermute(
            lax.slice_in_dim(block, block.shape[dim] - width, None, axis=dim), axis, forward
        )
        high = lax.ppermute(lax.slice_in_dim(block, 0, width, axis=dim), axis, backward)
        block = jnp.concatenate([low, block, high], axis=dim)
    return block


def from_behind(shard, axis, by):
    length = lax.axis_size(axis)
    pairs = [(i, i + by) for i in range(length) if 0 <= i + by < length]
    return lax.ppermute(shard, axis, pairs)


def advance(extended, east_wind, north_wind, spread):
    center = extended[:, :, 1:-1]
    western = extended[:, :, :-2]
    eastern = extended[:, :, 2:]
    zeros_row = jnp.zeros_like(center[:, :1])
    southern = jnp.concatenate([zeros_row, center[:, :-1]], axis=1)
    northern = jnp.concatenate([center[:, 1:], zeros_row], axis=1)
    east_wind = east_wind[None, :, :, None]
    north_wind = north_wind[None, :, :, None]
    spread = spread[None, :, :, None]
    transport = (
        jnp.maximum(east_wind, 0.0) * (center - western)
        + jnp.minimum(east_wind, 0.0) * (eastern - center)
        + jnp.maximum(north_wind, 0.0) * (center - southern)
        + jnp.minimum(north_wind, 0.0) * (northern - center)
    )
    return center - transport + spread * (eastern + western + northern + southern - 4.0 * center)


def propagate(state_field, winds, diffusivity):
    for substep in range(STEPS):
        extended = extended_2(state_field, (("lon", 2),), 1)
        state_field = advance(extended, winds[0, substep], winds[1, substep], diffusivity)
    return state_field


def relayout(block, reach_rows):
    row_count = block.shape[0]
    lat_count = block.shape[1]
    swapped = lax.all_to_all(block, "lon", split_axis=3, concat_axis=2, tiled=True)
    lon_count = swapped.shape[2]
    col_count = swapped.shape[3]
    block_count = lat_count // row_count
    device_index = lax.axis_index("lat")
    reach_blocks = min((reach_rows + row_count - 1) // row_count, block_count - 1)
    tile_blocks = swapped.reshape(row_count, block_count, row_count, lon_count, col_count)

    def piece_for(offset):
        target = jnp.clip(device_index + offset, 0, block_count - 1)
        return lax.dynamic_index_in_dim(tile_blocks, target, axis=1, keepdims=False)

    own_piece = piece_for(0)
    received = []
    for offset in range(-reach_blocks, reach_blocks + 1):
        if offset == 0:
            received.append(own_piece)
        else:
            received.append(from_behind(piece_for(offset), "lat", offset))
    window = jnp.stack(received[::-1], axis=0)
    padded = jnp.zeros(
        (block_count + 2 * reach_blocks, row_count, row_count, lon_count, col_count), jnp.float32
    )
    padded = lax.dynamic_update_slice_in_dim(padded, window, device_index, 0)
    regrouped = padded[reach_blocks : reach_blocks + block_count].reshape(
        lat_count, row_count, lon_count, col_count
    )
    return jnp.transpose(regrouped, (1, 0, 3, 2))


def per_device(covariance, winds, diffusivity, cutoff):
    row_count = covariance.shape[0]
    lat_count = covariance.shape[1]
    band_rows = lat_count // 4
    device_index = lax.axis_index("lat")
    lat_local = device_index * row_count + jnp.arange(row_count, dtype=jnp.int32)
    lat_all = jnp.arange(lat_count, dtype=jnp.int32)
    cut_local = lax.dynamic_slice_in_dim(cutoff, device_index * row_count, row_count)
    keep_first = jnp.abs(lat_all[None, :] - lat_local[:, None]) <= cutoff[None, :]
    keep_second = jnp.abs(lat_all[None, :] - lat_local[:, None]) <= cut_local[:, None]
    state_field = jnp.where(keep_first[:, :, None, None], covariance, 0.0)
    state_field = propagate(state_field, winds, diffusivity)
    state_field = relayout(state_field, band_rows + STEPS)
    state_field = propagate(state_field, winds, diffusivity)
    state_field = jnp.where(keep_second[:, :, None, None], state_field, 0.0)
    return relayout(state_field, band_rows)


def solution(mesh):
    in_specs = (P("lat", None, "lon", None), P(None, None, None, "lon"), P(None, "lon"), P())
    out_specs = P("lat", None, "lon", None)
    return jax.shard_map(
        per_device, mesh=mesh, in_specs=in_specs, out_specs=out_specs, check_vma=False
    )
```

profile of v0, /device:TPU:24, one launch (start us, length us, event | category | flops | bytes accessed | tf_op | source)
XLA Modules:
  0.0 880.4 jit_solution(16110254045664270610)
XLA Ops:
  28.5 10.3 %all-to-all-done = f32[8,1,16384]{2,1,0:T(1,128)S(1)} async-done(((f32[8,1,16384]{2,1,0:T(1,128)}), f32[8,1,16384]{2,1,0:T(1,128)S(1)}, u32[]{:S(2)}, u32[]{:S(2)}) %all-to-all-start) | async-done | bytes 524320 | tf_op jit(solution)/shard_map/all_to_all | solution.py:58
  44.4 8.4 constant_dynamic-slice_fusion.51
  54.4 21.2 %collective-permute-start.7 = (f32[1,1,128,16]{2,3,1,0:T(8,128)S(1)}, f32[1,1,128,16]{2,3,1,0:T(8,128)S(1)}, u32[]{:S(2)}, u32[]{:S(2)}) collective-permute-start(f32[1,1,128,16]{2,3,1,0:T(8,128)S(1)} %bitcast.330), channel_id=1, source_target_pairs={{0,144},{8,152},{16,160},{24,168},{32,176},{40,184},{48,192},{56,2... | collective-permute-start | bytes 24584 | tf_op jit(solution)/shard_map/ppermute | solution.py:26
  77.3 19.0 %collective-permute-start.8 = (f32[1,1,128,16]{2,3,1,0:T(8,128)S(1)}, f32[1,1,128,16]{2,3,1,0:T(8,128)S(1)}, u32[]{:S(2)}, u32[]{:S(2)}) collective-permute-start(f32[1,1,128,16]{2,3,1,0:T(8,128)S(1)} %bitcast.329), channel_id=1, source_target_pairs={{0,136},{8,144},{16,152},{24,160},{32,168},{40,176},{48,184},{56,1... | collective-permute-start | bytes 24584 | tf_op jit(solution)/shard_map/ppermute | solution.py:26
  100.8 8.6 collective-permute-start.10
  143.9 8.9 %constant_dynamic-slice_fusion.32 = (f32[1,1,1,128,16]{1,4,3,2,0:T(8,128)}, f32[1,1,1,128,16]{1,4,3,2,0:T(8,128)}, f32[1,1,1,128,16]{1,4,3,2,0:T(8,128)}, f32[1,...) fusion(f32[1,64,1,128,16]{1,4,3,2,0:T(8,128)S(1)} %bitcast.189,, ...), kind=kLoop, calls=%fused_computation.205 | loop fusion | bytes 294984 | tf_op jit(solution)/shard_map/jit(dynamic_index_in_dim)/dynamic_slice | solution.py:68
  248.6 8.7 collective-permute-start.29
  295.2 10.0 %collective-permute-start.30 = (f32[1,1,128,16]{2,3,1,0:T(8,128)S(1)}, f32[1,1,128,16]{2,3,1,0:T(8,128)S(1)}, u32[]{:S(2)}, u32[]{:S(2)}) collective-permute-start(f32[1,1,128,16]{2,3,1,0:T(8,128)S(1)} %bitcast.218), channel_id=1, source_target_pairs={{48,0},{56,8},{64,16},{72,24},{80,32},{88,40},{96,48},{104,56},{11... | collective-permute-start | bytes 24584 | tf_op jit(solution)/shard_map/ppermute | solution.py:26
  305.7 11.5 %collective-permute-start.31 = (f32[1,1,128,16]{2,3,1,0:T(8,128)S(1)}, f32[1,1,128,16]{2,3,1,0:T(8,128)S(1)}, u32[]{:S(2)}, u32[]{:S(2)}) collective-permute-start(f32[1,1,128,16]{2,3,1,0:T(8,128)S(1)} %bitcast.217), channel_id=1, source_target_pairs={{56,0},{64,8},{72,16},{80,24},{88,32},{96,40},{104,48},{112,56},{1... | collective-permute-start | bytes 24584 | tf_op jit(solution)/shard_map/ppermute | solution.py:26
  317.2 12.4 %collective-permute-start.32 = (f32[1,1,128,16]{2,3,1,0:T(8,128)S(1)}, f32[1,1,128,16]{2,3,1,0:T(8,128)S(1)}, u32[]{:S(2)}, u32[]{:S(2)}) collective-permute-start(f32[1,1,128,16]{2,3,1,0:T(8,128)S(1)} %bitcast.216), channel_id=1, source_target_pairs={{64,0},{72,8},{80,16},{88,24},{96,32},{104,40},{112,48},{120,56},{... | collective-permute-start | bytes 24584 | tf_op jit(solution)/shard_map/ppermute | solution.py:26
  329.6 10.3 %collective-permute-start.33 = (f32[1,1,128,16]{2,3,1,0:T(8,128)S(1)}, f32[1,1,128,16]{2,3,1,0:T(8,128)S(1)}, u32[]{:S(2)}, u32[]{:S(2)}) collective-permute-start(f32[1,1,128,16]{2,3,1,0:T(8,128)S(1)} %bitcast.215), channel_id=1, source_target_pairs={{72,0},{80,8},{88,16},{96,24},{104,32},{112,40},{120,48},{128,56},... | collective-permute-start | bytes 24584 | tf_op jit(solution)/shard_map/ppermute | solution.py:26
  357.7 13.2 %collective-permute-start.41 = (f32[1,1,128,16]{2,3,1,0:T(8,128)S(1)}, f32[1,1,128,16]{2,3,1,0:T(8,128)S(1)}, u32[]{:S(2)}, u32[]{:S(2)}) collective-permute-start(f32[1,1,128,16]{2,3,1,0:T(8,128)S(1)} %bitcast.199), channel_id=1, source_target_pairs={{136,0},{144,8},{152,16},{160,24},{168,32},{176,40},{184,48},{192,... | collective-permute-start | bytes 24584 | tf_op jit(solution)/shard_map/ppermute | solution.py:26
  371.0 19.0 %collective-permute-start.42 = (f32[1,1,128,16]{2,3,1,0:T(8,128)S(1)}, f32[1,1,128,16]{2,3,1,0:T(8,128)S(1)}, u32[]{:S(2)}, u32[]{:S(2)}) collective-permute-start(f32[1,1,128,16]{2,3,1,0:T(8,128)S(1)} %bitcast.198), channel_id=1, source_target_pairs={{144,0},{152,8},{160,16},{168,24},{176,32},{184,40},{192,48},{200,... | collective-permute-start | bytes 24584 | tf_op jit(solution)/shard_map/ppermute | solution.py:26
  390.0 19.0 %collective-permute-start.43 = (f32[1,1,128,16]{2,3,1,0:T(8,128)S(1)}, f32[1,1,128,16]{2,3,1,0:T(8,128)S(1)}, u32[]{:S(2)}, u32[]{:S(2)}) collective-permute-start(f32[1,1,128,16]{2,3,1,0:T(8,128)S(1)} %bitcast.197), channel_id=1, source_target_pairs={{152,0},{160,8},{168,16},{176,24},{184,32},{192,40},{200,48},{208,... | collective-permute-start | bytes 24584 | tf_op jit(solution)/shard_map/ppermute | solution.py:26
  409.0 9.1 %collective-permute-start.25 = (f32[1,1,128,16]{2,3,1,0:T(8,128)S(1)}, f32[1,1,128,16]{2,3,1,0:T(8,128)S(1)}, u32[]{:S(2)}, u32[]{:S(2)}) collective-permute-start(f32[1,1,128,16]{2,3,1,0:T(8,128)S(1)} %bitcast.265), channel_id=1, source_target_pairs={{8,0},{16,8},{24,16},{32,24},{40,32},{48,40},{56,48},{64,56},{72,6... | collective-permute-start | bytes 24584 | tf_op jit(solution)/shard_map/ppermute | solution.py:26
  482.8 23.8 %copy.588 = f32[39,1,1,128,16]{0,4,3,2,1:T(8,128)S(1)} copy(f32[39,1,1,128,16]{1,4,3,2,0:T(8,128)} %constant_dynamic-update-slice_fusion) | data formatting | bytes 638976 | tf_op jit(solution)/shard_map/stack | solution.py:77
  506.6 21.2 %dynamic_update_slice.6 = f32[102,1,1,128,16]{0,4,3,2,1:T(8,128)S(1)} dynamic-update-slice(f32[102,1,1,128,16]{0,4,3,2,1:T(8,128)S(1)} %broadcast_in_dim.38, f32[39,1,1,128,16]{0,4,3,2,1:T(8,128)S(1)} %copy.588, s32[]{:T(128)S(6)} %select_n.91, s32[]{:T(128)} %constant.241.clone.1, s32[]{:T(128)} %constant.241.clone.1, s32[]{:T(128)} %constant.241.clone.1, s32[]{:T(128)} %constant.241.clone.1) | dynamic-update-slice | bytes 638980 | tf_op jit(solution)/shard_map/dynamic_update_slice | solution.py:81
  547.2 14.6 %all_to_all.30 = f32[8,1,16384]{2,1,0:T(1,128)S(1)} all-to-all(f32[8,1,16384]{2,1,0:T(1,128)S(1)} %reshape.178), channel_id=1, replica_groups=mesh['lat'=64,'lon'=8] {'lon'}, dimensions={0} | all-to-all | bytes 1048576 | tf_op jit(solution)/shard_map/all_to_all | solution.py:58
  725.4 8.7 collective-permute-start.70
  735.8 12.0 %collective-permute-start.71 = (f32[1,1,128,16]{2,3,1,0:T(8,128)S(1)}, f32[1,1,128,16]{2,3,1,0:T(8,128)S(1)}, u32[]{:S(2)}, u32[]{:S(2)}) collective-permute-start(f32[1,1,128,16]{2,3,1,0:T(8,128)S(1)} %bitcast.320), channel_id=1, source_target_pairs={{48,0},{56,8},{64,16},{72,24},{80,32},{88,40},{96,48},{104,56},{11... | collective-permute-start | bytes 24584 | tf_op jit(solution)/shard_map/ppermute | solution.py:26
  755.9 9.7 %collective-permute-start.72 = (f32[1,1,128,16]{2,3,1,0:T(8,128)S(1)}, f32[1,1,128,16]{2,3,1,0:T(8,128)S(1)}, u32[]{:S(2)}, u32[]{:S(2)}) collective-permute-start(f32[1,1,128,16]{2,3,1,0:T(8,128)S(1)} %bitcast.311), channel_id=1, source_target_pairs={{56,0},{64,8},{72,16},{80,24},{88,32},{96,40},{104,48},{112,56},{1... | collective-permute-start | bytes 24584 | tf_op jit(solution)/shard_map/ppermute | solution.py:26
  765.6 12.4 %collective-permute-start.73 = (f32[1,1,128,16]{2,3,1,0:T(8,128)S(1)}, f32[1,1,128,16]{2,3,1,0:T(8,128)S(1)}, u32[]{:S(2)}, u32[]{:S(2)}) collective-permute-start(f32[1,1,128,16]{2,3,1,0:T(8,128)S(1)} %bitcast.304), channel_id=1, source_target_pairs={{64,0},{72,8},{80,16},{88,24},{96,32},{104,40},{112,48},{120,56},{... | collective-permute-start | bytes 24584 | tf_op jit(solution)/shard_map/ppermute | solution.py:26
  778.0 10.1 %collective-permute-start.74 = (f32[1,1,128,16]{2,3,1,0:T(8,128)S(1)}, f32[1,1,128,16]{2,3,1,0:T(8,128)S(1)}, u32[]{:S(2)}, u32[]{:S(2)}) collective-permute-start(f32[1,1,128,16]{2,3,1,0:T(8,128)S(1)} %bitcast.299), channel_id=1, source_target_pairs={{72,0},{80,8},{88,16},{96,24},{104,32},{112,40},{120,48},{128,56},... | collective-permute-start | bytes 24584 | tf_op jit(solution)/shard_map/ppermute | solution.py:26
  860.0 19.0 %copy.655 = f32[33,1,1,128,16]{3,4,0,2,1:T(8,128)S(1)} copy(f32[33,1,1,128,16]{1,4,3,2,0:T(8,128)} %constant_dynamic-update-slice_fusion.38) | data formatting | bytes 540672 | tf_op jit(solution)/shard_map/stack | solution.py:77
  (406 shorter events, 557.4 us)
Async XLA Ops:
  42.9 71.4 %collective-permute-start.6 = (f32[1,1,128,16]{2,3,1,0:T(8,128)S(1)}, f32[1,1,128,16]{2,3,1,0:T(8,128)S(1)}, u32[]{:S(2)}, u32[]{:S(2)}) collective-permute-start(f32[1,1,128,16]{2,3,1,0:T(8,128)S(1)} %bitcast.315), channel_id=1, source_target_pairs={{0,152},{8,160},{16,168},{24,176},{32,184},{40,192},{48,200},{56,2... | collective-permute-start | bytes 24584 | tf_op jit(solution)/shard_map/ppermute | solution.py:26
  54.4 61.8 %collective-permute-start.7 = (f32[1,1,128,16]{2,3,1,0:T(8,128)S(1)}, f32[1,1,128,16]{2,3,1,0:T(8,128)S(1)}, u32[]{:S(2)}, u32[]{:S(2)}) collective-permute-start(f32[1,1,128,16]{2,3,1,0:T(8,128)S(1)} %bitcast.330), channel_id=1, source_target_pairs={{0,144},{8,152},{16,160},{24,168},{32,176},{40,184},{48,192},{56,2... | collective-permute-start | bytes 24584 | tf_op jit(solution)/shard_map/ppermute | solution.py:26
  130.2 61.2 %collective-permute-start.14 = (f32[1,1,128,16]{2,3,1,0:T(8,128)}, f32[1,1,128,16]{2,3,1,0:T(8,128)S(1)}, u32[]{:S(2)}, u32[]{:S(2)}) collective-permute-start(f32[1,1,128,16]{2,3,1,0:T(8,128)} %bitcast.32), channel_id=1, source_target_pairs={{0,88},{8,96},{16,104},{24,112},{32,120},{40,128},{48,136},{56,144... | collective-permute-start | bytes 24584 | tf_op jit(solution)/shard_map/ppermute | solution.py:26
  133.3 60.1 %collective-permute-start.15 = (f32[1,1,128,16]{2,3,1,0:T(8,128)}, f32[1,1,128,16]{2,3,1,0:T(8,128)S(1)}, u32[]{:S(2)}, u32[]{:S(2)}) collective-permute-start(f32[1,1,128,16]{2,3,1,0:T(8,128)} %bitcast.34), channel_id=1, source_target_pairs={{0,80},{8,88},{16,96},{24,104},{32,112},{40,120},{48,128},{56,136}... | collective-permute-start | bytes 24584 | tf_op jit(solution)/shard_map/ppermute | solution.py:26
  135.2 60.1 %collective-permute-start.16 = (f32[1,1,128,16]{2,3,1,0:T(8,128)S(1)}, f32[1,1,128,16]{2,3,1,0:T(8,128)S(1)}, u32[]{:S(2)}, u32[]{:S(2)}) collective-permute-start(f32[1,1,128,16]{2,3,1,0:T(8,128)S(1)} %bitcast.245), channel_id=1, source_target_pairs={{0,72},{8,80},{16,88},{24,96},{32,104},{40,112},{48,120},{56,128},... | collective-permute-start | bytes 24584 | tf_op jit(solution)/shard_map/ppermute | solution.py:26
  137.2 60.1 %collective-permute-start.17 = (f32[1,1,128,16]{2,3,1,0:T(8,128)S(1)}, f32[1,1,128,16]{2,3,1,0:T(8,128)S(1)}, u32[]{:S(2)}, u32[]{:S(2)}) collective-permute-start(f32[1,1,128,16]{2,3,1,0:T(8,128)S(1)} %bitcast.239), channel_id=1, source_target_pairs={{0,64},{8,72},{16,80},{24,88},{32,96},{40,104},{48,112},{56,120},{... | collective-permute-start | bytes 24584 | tf_op jit(solution)/shard_map/ppermute | solution.py:26
  139.1 60.7 %collective-permute-start.18 = (f32[1,1,128,16]{2,3,1,0:T(8,128)S(1)}, f32[1,1,128,16]{2,3,1,0:T(8,128)S(1)}, u32[]{:S(2)}, u32[]{:S(2)}) collective-permute-start(f32[1,1,128,16]{2,3,1,0:T(8,128)S(1)} %bitcast.237), channel_id=1, source_target_pairs={{0,56},{8,64},{16,72},{24,80},{32,88},{40,96},{48,104},{56,112},{6... | collective-permute-start | bytes 24584 | tf_op jit(solution)/shard_map/ppermute | solution.py:26
  199.8 48.8 %collective-permute-start.23 = (f32[1,1,128,16]{2,3,1,0:T(8,128)S(1)}, f32[1,1,128,16]{2,3,1,0:T(8,128)S(1)}, u32[]{:S(2)}, u32[]{:S(2)}) collective-permute-start(f32[1,1,128,16]{2,3,1,0:T(8,128)S(1)} %bitcast.236), channel_id=1, source_target_pairs={{0,16},{8,24},{16,32},{24,40},{32,48},{40,56},{48,64},{56,72},{64,... | collective-permute-start | bytes 24584 | tf_op jit(solution)/shard_map/ppermute | solution.py:26
  218.0 77.2 %collective-permute-start.24 = (f32[1,1,128,16]{2,3,1,0:T(8,128)S(1)}, f32[1,1,128,16]{2,3,1,0:T(8,128)S(1)}, u32[]{:S(2)}, u32[]{:S(2)}) collective-permute-start(f32[1,1,128,16]{2,3,1,0:T(8,128)S(1)} %bitcast.225), channel_id=1, source_target_pairs={{0,8},{8,16},{16,24},{24,32},{32,40},{40,48},{48,56},{56,64},{64,7... | collective-permute-start | bytes 24584 | tf_op jit(solution)/shard_map/ppermute | solution.py:26
  222.6 83.2 %collective-permute-start.26 = (f32[1,1,128,16]{2,3,1,0:T(8,128)S(1)}, f32[1,1,128,16]{2,3,1,0:T(8,128)S(1)}, u32[]{:S(2)}, u32[]{:S(2)}) collective-permute-start(f32[1,1,128,16]{2,3,1,0:T(8,128)S(1)} %bitcast.223), channel_id=1, source_target_pairs={{16,0},{24,8},{32,16},{40,24},{48,32},{56,40},{64,48},{72,56},{80,... | collective-permute-start | bytes 24584 | tf_op jit(solution)/shard_map/ppermute | solution.py:26
  231.1 86.1 %collective-permute-start.27 = (f32[1,1,128,16]{2,3,1,0:T(8,128)S(1)}, f32[1,1,128,16]{2,3,1,0:T(8,128)S(1)}, u32[]{:S(2)}, u32[]{:S(2)}) collective-permute-start(f32[1,1,128,16]{2,3,1,0:T(8,128)S(1)} %bitcast.222), channel_id=1, source_target_pairs={{24,0},{32,8},{40,16},{48,24},{56,32},{64,40},{72,48},{80,56},{88,... | collective-permute-start | bytes 24584 | tf_op jit(solution)/shard_map/ppermute | solution.py:26
  239.4 90.2 %collective-permute-start.28 = (f32[1,1,128,16]{2,3,1,0:T(8,128)S(1)}, f32[1,1,128,16]{2,3,1,0:T(8,128)S(1)}, u32[]{:S(2)}, u32[]{:S(2)}) collective-permute-start(f32[1,1,128,16]{2,3,1,0:T(8,128)S(1)} %bitcast.220), channel_id=1, source_target_pairs={{32,0},{40,8},{48,16},{56,24},{64,32},{72,40},{80,48},{88,56},{96,... | collective-permute-start | bytes 24584 | tf_op jit(solution)/shard_map/ppermute | solution.py:26
  248.6 91.3 %collective-permute-start.29 = (f32[1,1,128,16]{2,3,1,0:T(8,128)S(1)}, f32[1,1,128,16]{2,3,1,0:T(8,128)S(1)}, u32[]{:S(2)}, u32[]{:S(2)}) collective-permute-start(f32[1,1,128,16]{2,3,1,0:T(8,128)S(1)} %bitcast.219), channel_id=1, source_target_pairs={{40,0},{48,8},{56,16},{64,24},{72,32},{80,40},{88,48},{96,56},{104... | collective-permute-start | bytes 24584 | tf_op jit(solution)/shard_map/ppermute | solution.py:26
  295.2 48.5 %collective-permute-start.30 = (f32[1,1,128,16]{2,3,1,0:T(8,128)S(1)}, f32[1,1,128,16]{2,3,1,0:T(8,128)S(1)}, u32[]{:S(2)}, u32[]{:S(2)}) collective-permute-start(f32[1,1,128,16]{2,3,1,0:T(8,128)S(1)} %bitcast.218), channel_id=1, source_target_pairs={{48,0},{56,8},{64,16},{72,24},{80,32},{88,40},{96,48},{104,56},{11... | collective-permute-start | bytes 24584 | tf_op jit(solution)/shard_map/ppermute | solution.py:26
  352.4 56.6 %collective-permute-start.39 = (f32[1,1,128,16]{2,3,1,0:T(8,128)S(1)}, f32[1,1,128,16]{2,3,1,0:T(8,128)S(1)}, u32[]{:S(2)}, u32[]{:S(2)}) collective-permute-start(f32[1,1,128,16]{2,3,1,0:T(8,128)S(1)} %bitcast.209), channel_id=1, source_target_pairs={{120,0},{128,8},{136,16},{144,24},{152,32},{160,40},{168,48},{176,... | collective-permute-start | bytes 24584 | tf_op jit(solution)/shard_map/ppermute | solution.py:26
  356.4 79.4 %collective-permute-start.40 = (f32[1,1,128,16]{2,3,1,0:T(8,128)S(1)}, f32[1,1,128,16]{2,3,1,0:T(8,128)S(1)}, u32[]{:S(2)}, u32[]{:S(2)}) collective-permute-start(f32[1,1,128,16]{2,3,1,0:T(8,128)S(1)} %bitcast.200), channel_id=1, source_target_pairs={{128,0},{136,8},{144,16},{152,24},{160,32},{168,40},{176,48},{184,... | collective-permute-start | bytes 24584 | tf_op jit(solution)/shard_map/ppermute | solution.py:26
  357.7 79.6 %collective-permute-start.41 = (f32[1,1,128,16]{2,3,1,0:T(8,128)S(1)}, f32[1,1,128,16]{2,3,1,0:T(8,128)S(1)}, u32[]{:S(2)}, u32[]{:S(2)}) collective-permute-start(f32[1,1,128,16]{2,3,1,0:T(8,128)S(1)} %bitcast.199), channel_id=1, source_target_pairs={{136,0},{144,8},{152,16},{160,24},{168,32},{176,40},{184,48},{192,... | collective-permute-start | bytes 24584 | tf_op jit(solution)/shard_map/ppermute | solution.py:26
  371.0 67.7 %collective-permute-start.42 = (f32[1,1,128,16]{2,3,1,0:T(8,128)S(1)}, f32[1,1,128,16]{2,3,1,0:T(8,128)S(1)}, u32[]{:S(2)}, u32[]{:S(2)}) collective-permute-start(f32[1,1,128,16]{2,3,1,0:T(8,128)S(1)} %bitcast.198), channel_id=1, source_target_pairs={{144,0},{152,8},{160,16},{168,24},{176,32},{184,40},{192,48},{200,... | collective-permute-start | bytes 24584 | tf_op jit(solution)/shard_map/ppermute | solution.py:26
  390.0 50.1 %collective-permute-start.43 = (f32[1,1,128,16]{2,3,1,0:T(8,128)S(1)}, f32[1,1,128,16]{2,3,1,0:T(8,128)S(1)}, u32[]{:S(2)}, u32[]{:S(2)}) collective-permute-start(f32[1,1,128,16]{2,3,1,0:T(8,128)S(1)} %bitcast.197), channel_id=1, source_target_pairs={{152,0},{160,8},{168,16},{176,24},{184,32},{192,40},{200,48},{208,... | collective-permute-start | bytes 24584 | tf_op jit(solution)/shard_map/ppermute | solution.py:26
  701.5 54.4 %collective-permute-start.67 = (f32[1,1,128,16]{2,3,1,0:T(8,128)S(1)}, f32[1,1,128,16]{2,3,1,0:T(8,128)S(1)}, u32[]{:S(2)}, u32[]{:S(2)}) collective-permute-start(f32[1,1,128,16]{2,3,1,0:T(8,128)S(1)} %bitcast.328), channel_id=1, source_target_pairs={{16,0},{24,8},{32,16},{40,24},{48,32},{56,40},{64,48},{72,56},{80,... | collective-permute-start | bytes 24584 | tf_op jit(solution)/shard_map/ppermute | solution.py:26
  707.9 57.7 %collective-permute-start.68 = (f32[1,1,128,16]{2,3,1,0:T(8,128)S(1)}, f32[1,1,128,16]{2,3,1,0:T(8,128)S(1)}, u32[]{:S(2)}, u32[]{:S(2)}) collective-permute-start(f32[1,1,128,16]{2,3,1,0:T(8,128)S(1)} %bitcast.326), channel_id=1, source_target_pairs={{24,0},{32,8},{40,16},{48,24},{56,32},{64,40},{72,48},{80,56},{88,... | collective-permute-start | bytes 24584 | tf_op jit(solution)/shard_map/ppermute | solution.py:26
  716.4 61.6 %collective-permute-start.69 = (f32[1,1,128,16]{2,3,1,0:T(8,128)S(1)}, f32[1,1,128,16]{2,3,1,0:T(8,128)S(1)}, u32[]{:S(2)}, u32[]{:S(2)}) collective-permute-start(f32[1,1,128,16]{2,3,1,0:T(8,128)S(1)} %bitcast.324), channel_id=1, source_target_pairs={{32,0},{40,8},{48,16},{56,24},{64,32},{72,40},{80,48},{88,56},{96,... | collective-permute-start | bytes 24584 | tf_op jit(solution)/shard_map/ppermute | solution.py:26
  725.4 62.7 %collective-permute-start.70 = (f32[1,1,128,16]{2,3,1,0:T(8,128)S(1)}, f32[1,1,128,16]{2,3,1,0:T(8,128)S(1)}, u32[]{:S(2)}, u32[]{:S(2)}) collective-permute-start(f32[1,1,128,16]{2,3,1,0:T(8,128)S(1)} %bitcast.322), channel_id=1, source_target_pairs={{40,0},{48,8},{56,16},{64,24},{72,32},{80,40},{88,48},{96,56},{104... | collective-permute-start | bytes 24584 | tf_op jit(solution)/shard_map/ppermute | solution.py:26
  735.8 54.4 %collective-permute-start.71 = (f32[1,1,128,16]{2,3,1,0:T(8,128)S(1)}, f32[1,1,128,16]{2,3,1,0:T(8,128)S(1)}, u32[]{:S(2)}, u32[]{:S(2)}) collective-permute-start(f32[1,1,128,16]{2,3,1,0:T(8,128)S(1)} %bitcast.320), channel_id=1, source_target_pairs={{48,0},{56,8},{64,16},{72,24},{80,32},{88,40},{96,48},{104,56},{11... | collective-permute-start | bytes 24584 | tf_op jit(solution)/shard_map/ppermute | solution.py:26
  (61 other events, 1408.4 us)
where the time goes:
time: 895 us; the launch traced here: 880 us
  local copies, waits for them, and re-layouts  449 us (50%)
  starting transfers between devices  380 us (42%)
  waiting for transfers between devices  20.2 us (2%)
  other arithmetic  14.6 us (2%)
  blocking collectives  14.6 us (2%)
    ppermute x70, starting transfers between devices, from_behind(): return lax.ppermute(shard, axis, pairs)  358 us
    unnamed x77, local copies, waits for them, and re-layouts  144 us
    dynamic_slice x76, local copies, waits for them, and re-layouts, piece_for(): return lax.dynamic_index_in_dim(tile_blocks, target, axis=1, keepdims=False)  142 us
    another operation x74, local copies, waits for them, and re-layouts, relayout(): window = jnp.stack(received[::-1], axis=0)  136 us
    dynamic_update_slice x2, local copies, waits for them, and re-layouts, relayout(): padded = lax.dynamic_update_slice_in_dim(padded, window, device_index, 0)  21.2 us
  transfers between devices with their start and end apart: 83, of which 8 were waited for; matrix products, arithmetic and copies ran while one was open for 28% of the time, Pallas kernels for 0%

commit v1 on v0

v1 whole, which is shorter than its diff:
```python
import functools

import jax
import jax.numpy as jnp
from jax import lax
from jax.experimental import pallas as pl
from jax.experimental.pallas import tpu as pltpu
from jax.sharding import PartitionSpec as P

MESH = pl.DeviceIdType.MESH
NLAT = 64
WIDE = 16
OFF = 20
ROWS = 2 * OFF + 1
B1 = (-17, -10, -3, 4, 11, 18)
B2 = (-17, -14, -7, 0, 7, 13, 18)
B3 = (-16, -15, -8, -1, 6, 12, 17)
HALO = 8


def pieces(bounds, low, high):
    return [(max(a, low), min(b, high + 1)) for a, b in zip(bounds[:-1], bounds[1:])]


def kernel(lats, lons, x_ref, winds_ref, diff_ref, cut_ref, out_ref,
           xv, xm, wv, dv, l1, r1, l2, r2, l3, r3, e0, e1, e2, h1, h2, co, tab, gath,
           load_sem, s_send, s_recv, p_send, p_recv, t_send, t_recv, g_send, g_recv):
    j = lax.axis_index("lat")
    b = lax.axis_index("lon")
    up, down = lax.rem(j + 1, lats), lax.rem(j + lats - 1, lats)
    east, west = lax.rem(b + 1, lons), lax.rem(b + lons - 1, lons)

    barrier = pltpu.get_barrier_semaphore()
    pl.semaphore_signal(barrier, inc=1, device_id=(up, b), device_id_type=MESH)
    pl.semaphore_signal(barrier, inc=1, device_id=(down, b), device_id_type=MESH)
    for d in range(1, lons):
        pl.semaphore_signal(barrier, inc=1, device_id=(j, lax.rem(b + d, lons)), device_id_type=MESH)

    load_x = pltpu.make_async_copy(x_ref.at[0], xv, load_sem.at[0])
    load_w = pltpu.make_async_copy(winds_ref, wv, load_sem.at[1])
    load_d = pltpu.make_async_copy(diff_ref, dv, load_sem.at[2])
    load_x.start()
    load_w.start()
    load_d.start()

    def lat_of(n):
        return lax.rem(j + n + (NLAT - OFF), NLAT)

    def keep(n):
        cut = cut_ref[lat_of(n)]
        inside = jnp.logical_and(j + n >= OFF, j + n < NLAT + OFF)
        near = jnp.logical_and(n <= OFF + cut, n + cut >= OFF)
        return jnp.where(jnp.logical_and(inside, near), 1.0, 0.0).astype(jnp.float32)

    zero = jnp.zeros((16, 128), jnp.float32)
    zero_e = jnp.zeros((2 * HALO + 16, 128), jnp.float32)
    for r in (-17, 17):
        xm[r + OFF] = zero
    for r in (16, 17):
        l1[r + OFF] = zero
        r1[-r + OFF] = zero
    for r in (18, 19, 20):
        e0[r + OFF] = zero_e
        e0[-r + OFF] = zero_e
    for r in (19, 20):
        e1[r + OFF] = zero_e
        e1[-r + OFF] = zero_e

    load_x.wait()

    @pl.loop(OFF - WIDE, OFF + WIDE + 1)
    def _(n):
        xm[n] = xv[lat_of(n)] * keep(n)

    pl.semaphore_wait(barrier, 2 + lons - 1)

    def exchange(level, bounds, index, source, from_down, from_up, low, high):
        a, e = pieces(bounds, low, high)[index]
        to_up = pltpu.make_async_remote_copy(
            source.at[pl.ds(a + 1 + OFF, e - a)], from_down.at[pl.ds(a + OFF, e - a)],
            s_send.at[level, 0, index], s_recv.at[level, 0, index], device_id=(up, b), device_id_type=MESH)
        a, e = pieces(bounds, -high, -low)[index]
        to_down = pltpu.make_async_remote_copy(
            source.at[pl.ds(a - 1 + OFF, e - a)], from_up.at[pl.ds(a + OFF, e - a)],
            s_send.at[level, 1, index], s_recv.at[level, 1, index], device_id=(down, b), device_id_type=MESH)
        return to_up, to_down

    level1 = [exchange(0, B1, n, xm, l1, r1, -17, 15) for n in range(len(B1) - 1)]
    level2 = [exchange(1, B2, n, h1, l2, r2, -17, 17) for n in range(len(B2) - 1)]
    level3 = [exchange(2, B3, n, h2, l3, r3, -16, 16) for n in range(len(B3) - 1)]

    def begin(copies):
        for copy in copies:
            copy.start()

    for copies in level1:
        begin(copies)

    load_w.wait()
    load_d.wait()
    fields = [wv.at[c, s] for c in range(2) for s in range(3)] + [dv]
    lane = lax.broadcasted_iota(jnp.int32, (NLAT, 128), 1)
    sub = lax.broadcasted_iota(jnp.int32, (NLAT, 128), 0)
    turn = jnp.where(lane == sub - j + OFF, 1.0, 0.0).astype(jnp.float32)
    lane = lax.broadcasted_iota(jnp.int32, (16, 128), 1)
    sub = lax.broadcasted_iota(jnp.int32, (16, 128), 0)
    place = jnp.where(lane == sub + b * 16, 1.0, 0.0).astype(jnp.float32)
    mine = []
    for n, f in enumerate(fields):
        table = jnp.dot(f[...], turn, precision=lax.Precision.HIGHEST, preferred_element_type=jnp.float32)
        tab[n, HALO:HALO + 16, :] = table
        mine.append(jnp.sum(table[:, OFF:OFF + 1] * place, axis=0, keepdims=True))
    mine.append(jnp.zeros((1, 128), jnp.float32))
    gath[b] = jnp.concatenate(mine, axis=0)
    gathers = []
    for d in range(1, lons):
        copy = pltpu.make_async_remote_copy(
            gath.at[b], gath.at[b], g_send.at[d - 1], g_recv.at[d - 1],
            device_id=(j, lax.rem(b + d, lons)), device_id_type=MESH)
        copy.start()
        gathers.append(copy)

    lo, hi = pl.ds(0, HALO), pl.ds(HALO + 16, HALO)
    first, last = pl.ds(HALO, HALO), pl.ds(16, HALO)

    def halo(ref, send, recv, rows=None):
        rows = slice(None) if rows is None else rows
        to_east = pltpu.make_async_remote_copy(
            ref.at[rows, last], ref.at[rows, lo], send.at[0], recv.at[0],
            device_id=(j, east), device_id_type=MESH)
        to_west = pltpu.make_async_remote_copy(
            ref.at[rows, first], ref.at[rows, hi], send.at[1], recv.at[1],
            device_id=(j, west), device_id_type=MESH)
        return to_east, to_west

    tables = halo(tab, t_send, t_recv)
    begin(tables)

    @pl.loop(OFF + WIDE + 1, OFF + NLAT - WIDE)
    def _(n):
        out_ref[0, lat_of(n)] = zero

    for copy in gathers:
        copy.wait_recv()
    whole = gath[0]
    for d in range(1, lons):
        whole = whole + gath[d]
    k = whole[6:7]
    open_down = jnp.where(j == 0, 0.0, 1.0).astype(jnp.float32)
    open_up = jnp.where(j == NLAT - 1, 0.0, 1.0).astype(jnp.float32)

    def second(step, center, lower, upper):
        u, v = whole[step:step + 1], whole[3 + step:4 + step]
        c_w, c_e = k + jnp.maximum(u, 0.0), k - jnp.minimum(u, 0.0)
        c_s, c_n = k + jnp.maximum(v, 0.0), k - jnp.minimum(v, 0.0)
        c_0 = 1.0 - (c_w + c_e) - (c_s + c_n)
        c_s, c_n = c_s * open_down, c_n * open_up
        return (c_0 * center + c_w * pltpu.roll(center, 1, 1) + c_e * pltpu.roll(center, 127, 1)
                + c_s * lower + c_n * upper)

    def loop(a, e, body):
        def run(n, carry):
            body(n)
            return carry
        lax.fori_loop(a + OFF, e + OFF, run, 0)

    def do_g1(index):
        for copy in level1[index]:
            copy.wait_recv()
        a, e = B1[index], B1[index + 1]

        def body(n):
            e0[n, HALO:HALO + 16, :] = second(0, xm[n], l1[n], r1[n])
        loop(a, e, body)
        begin(halos[index])

    halos = [halo(e0, p_send.at[n], p_recv.at[n], pl.ds(B1[n] + OFF, B1[n + 1] - B1[n])) for n in range(len(B1) - 1)]

    def do_coefficients(a, e):
        for r in range(a, e):
            at = slice(r + OFF, r + OFF + 1)
            k_r = jnp.broadcast_to(tab[6, :, at], zero_e.shape)
            for s in range(3):
                u = jnp.broadcast_to(tab[s, :, at], zero_e.shape)
                v = jnp.broadcast_to(tab[3 + s, :, at], zero_e.shape)
                c_w, c_e = k_r + jnp.maximum(u, 0.0), k_r - jnp.minimum(u, 0.0)
                c_s, c_n = k_r + jnp.maximum(v, 0.0), k_r - jnp.minimum(v, 0.0)
                co[s, 0, r + OFF] = 1.0 - (c_w + c_e) - (c_s + c_n)
                co[s, 1, r + OFF] = c_w
                co[s, 2, r + OFF] = c_e
                co[s, 3, r + OFF] = c_s
                co[s, 4, r + OFF] = c_n

    def first_step(step, source, store, a, e):
        def body(n):
            center = source[n]
            store(n, co[step, 0, n] * center + co[step, 1, n] * pltpu.roll(center, 1, 0)
                  + co[step, 2, n] * pltpu.roll(center, 2 * HALO + 15, 0)
                  + co[step, 3, n] * source[n - 1] + co[step, 4, n] * source[n + 1])
        loop(a, e, body)

    def store_1(n, value):
        e1[n] = value

    def store_2(n, value):
        e2[n] = value

    def store_3(n, value):
        h1[n] = value[HALO:HALO + 16]

    done = [-18, -19, -18]

    def do_a1(end):
        for step, (source, store, limit, ahead) in enumerate(
                ((e0, store_1, 19, 2), (e1, store_2, 20, 1), (e2, store_3, 19, 0))):
            stop = min(end + ahead, limit)
            first_step(step, source, store, done[step], stop)
            done[step] = stop

    def do_h2(index):
        for copy in level2[index]:
            copy.wait_recv()

        def body(n):
            h2[n] = second(1, h1[n], l2[n], r2[n])
        loop(B2[index], B2[index + 1], body)

    def do_out(index):
        for copy in level3[index]:
            copy.wait_recv()

        def body(n):
            out_ref[0, lat_of(n)] = second(2, h2[n], l3[n], r3[n]) * keep(n)
        loop(B3[index], B3[index + 1], body)

    def wait_halo(index):
        for copy in halos[index]:
            copy.wait_recv()

    do_g1(0)
    for copy in tables:
        copy.wait_recv()
    do_coefficients(-19, 0)
    do_g1(1)
    do_coefficients(0, 20)

    def a1_for(index):
        do_a1(B2[index + 1] + 1)
        begin(level2[index])

    wait_halo(0)
    a1_for(0)
    do_g1(2)
    wait_halo(1)
    a1_for(1)
    do_g1(3)
    wait_halo(2)
    a1_for(2)
    do_g1(4)
    wait_halo(3)
    a1_for(3)
    wait_halo(4)
    a1_for(4)
    a1_for(5)
    for n in range(len(B2) - 1):
        do_h2(n)
        begin(level3[n])
    for n in range(len(B3) - 1):
        do_out(n)

    for copies in level1 + level2 + level3 + halos + [tables] + [gathers]:
        for copy in copies:
            copy.wait_send()


def per_device(covariance, winds, diffusivity, cutoff):
    lats, lons = lax.axis_size("lat"), lax.axis_size("lon")
    vm = lambda *shape: pltpu.VMEM(shape, jnp.float32)
    dma = lambda *shape: pltpu.SemaphoreType.DMA(shape)
    block = (ROWS, 16, 128)
    ext = (ROWS, 16 + 2 * HALO, 128)
    most = max(len(B1), len(B2), len(B3)) - 1
    return pl.pallas_call(
        functools.partial(kernel, lats, lons),
        out_shape=jax.ShapeDtypeStruct(covariance.shape, jnp.float32),
        in_specs=[pl.BlockSpec(memory_space=pl.ANY)] * 3 + [pl.BlockSpec(memory_space=pltpu.SMEM)],
        out_specs=pl.BlockSpec(memory_space=pltpu.VMEM),
        scratch_shapes=[
            vm(NLAT, 16, 128), vm(*block), vm(2, 3, 16, NLAT), vm(16, NLAT),
            vm(*block), vm(*block), vm(*block), vm(*block), vm(*block), vm(*block),
            vm(*ext), vm(*ext), vm(*ext), vm(*block), vm(*block),
            vm(3, 5, *ext), vm(7, 16 + 2 * HALO, 128), vm(lons, 8, 128),
            dma(3), dma(3, 2, most), dma(3, 2, most), dma(len(B1) - 1, 2), dma(len(B1) - 1, 2),
            dma(2), dma(2), dma(lons - 1), dma(lons - 1),
        ],
        compiler_params=pltpu.CompilerParams(
            collective_id=0, has_side_effects=True, vmem_limit_bytes=40 * 1024 * 1024),
        cost_estimate=pl.CostEstimate(flops=20_000_000, bytes_accessed=1_500_000, transcendentals=0),
    )(covariance, jnp.transpose(winds, (0, 1, 3, 2)), jnp.transpose(diffusivity), cutoff)


def solution(mesh):
    in_specs = (P("lat", None, "lon", None), P(None, None, None, "lon"), P(None, "lon"), P())
    out_specs = P("lat", None, "lon", None)
    return jax.shard_map(
        per_device, mesh=mesh, in_specs=in_specs, out_specs=out_specs, check_vma=False
    )
```

time: 895 us -> 46.4 us (0.05)
  the two profiles are of different devices: /device:TPU:24 before, /device:TPU:1 now
where the time goes in v1:
time: 46.4 us; the launch traced here: 46.1 us
  Pallas kernels  42.1 us (91%)
  local copies, waits for them, and re-layouts  3.99 us (9%)
    pallas_call x1, Pallas kernels, per_device(): pl.pallas_call(functools.partial(kernel, lats, lons), out_shape=jax.Shape...  42.1 us
    unnamed x9, local copies, waits for them, and re-layouts  3.99 us

profile of v1, /device:TPU:1, one launch (start us, length us, event | category | flops | bytes accessed | tf_op | source)
XLA Modules:
  0.0 46.1 jit_solution(17414267554154789259)
XLA Ops:
  0.0 0.0 copy-start.3
  0.0 0.7 %copy-done.3 = s32[64]{0:T(128)S(1)} copy-done((s32[64]{0:T(128)S(1)}, s32[64]{0:T(128)}, u32[]{:S(2)}) %copy-start.3) | copy-done | bytes 280
  0.7 0.0 copy-start
  0.7 1.0 %copy-done = f32[1,64,16,128]{3,2,1,0:T(8,128)S(1)} copy-done((f32[1,64,16,128]{3,2,1,0:T(8,128)S(1)}, f32[1,64,16,128]{3,2,1,0:T(8,128)}, u32[]{:S(2)}) %copy-start) | copy-done | bytes 524312
  1.7 0.0 copy-start.1
  1.7 0.8 %copy-done.1 = f32[2,3,64,16]{2,3,1,0:T(8,128)S(1)} copy-done((f32[2,3,64,16]{2,3,1,0:T(8,128)S(1)}, f32[2,3,64,16]{2,3,1,0:T(8,128)}, u32[]{:S(2)}) %copy-start.1) | copy-done | bytes 24600
  2.5 0.0 copy-start.2
  2.5 0.7 %copy-done.2 = f32[64,16]{0,1:T(8,128)S(1)} copy-done((f32[64,16]{0,1:T(8,128)S(1)}, f32[64,16]{0,1:T(8,128)}, u32[]{:S(2)}) %copy-start.2) | copy-done | bytes 4120
  3.2 42.1 %shard_map.46 = f32[1,64,16,128]{3,2,1,0:T(8,128)S(1)} custom-call(f32[1,64,16,128]{3,2,1,0:T(8,128)S(1)} %copy-done, f32[2,3,16,64]{3,2,1,0:T(8,128)S(1)} %bitcast.2, f32[16,64]{1,0:T(8,128)S(1)} %bitcast.3, s32[64]{0:T(128)S(1)} %copy-done.3), custom_call_target="tpu_custom_call" | custom-call | flops 20000000 | bytes 1500000 | tf_op jit(solution)/shard_map/pallas_call | solution.py:283
  45.3 0.8 %copy.6 = f32[1,64,16,128]{3,2,1,0:T(8,128)} copy(f32[1,64,16,128]{3,2,1,0:T(8,128)S(1)} %shard_map.46) | data formatting | bytes 1048576
Async XLA Ops:
  0.0 0.7 %copy-start.3 = (s32[64]{0:T(128)S(1)}, s32[64]{0:T(128)}, u32[]{:S(2)}) copy-start(s32[64]{0:T(128)} %cut_ref.1) | copy-start | bytes 772
  0.7 1.0 %copy-start = (f32[1,64,16,128]{3,2,1,0:T(8,128)S(1)}, f32[1,64,16,128]{3,2,1,0:T(8,128)}, u32[]{:S(2)}) copy-start(f32[1,64,16,128]{3,2,1,0:T(8,128)} %x_ref.1) | copy-start | bytes 1572868
  1.7 0.8 %copy-start.1 = (f32[2,3,64,16]{2,3,1,0:T(8,128)S(1)}, f32[2,3,64,16]{2,3,1,0:T(8,128)}, u32[]{:S(2)}) copy-start(f32[2,3,64,16]{2,3,1,0:T(8,128)} %param.5) | copy-start | bytes 73732
  2.5 0.7 %copy-start.2 = (f32[64,16]{0,1:T(8,128)S(1)}, f32[64,16]{0,1:T(8,128)}, u32[]{:S(2)}) copy-start(f32[64,16]{0,1:T(8,128)} %param.6) | copy-start | bytes 12292

commit v2 on v1

--- a/solution.py
+++ b/solution.py
@@ -22,24 +22,33 @@
     return [(max(a, low), min(b, high + 1)) for a, b in zip(bounds[:-1], bounds[1:])]
 
 
-def kernel(lats, lons, x_ref, winds_ref, diff_ref, cut_ref, out_ref,
-           xv, xm, wv, dv, l1, r1, l2, r2, l3, r3, e0, e1, e2, h1, h2, co, tab, gath,
+def kernel(lats, lons, x_ref, winds_ref, diff_ref, cutoff_ref, out_ref,
+           cut_ref, xv, xm, wv, dv, l1, r1, l2, r2, l3, r3, e0, e1, e2, h1, h2, co, tab, gath,
            load_sem, s_send, s_recv, p_send, p_recv, t_send, t_recv, g_send, g_recv):
     j = lax.axis_index("lat")
     b = lax.axis_index("lon")
     up, down = lax.rem(j + 1, lats), lax.rem(j + lats - 1, lats)
+    has_up, has_down = j < lats - 1, j > 0
     east, west = lax.rem(b + 1, lons), lax.rem(b + lons - 1, lons)
 
     barrier = pltpu.get_barrier_semaphore()
-    pl.semaphore_signal(barrier, inc=1, device_id=(up, b), device_id_type=MESH)
-    pl.semaphore_signal(barrier, inc=1, device_id=(down, b), device_id_type=MESH)
+    @pl.when(has_up)
+    def _():
+        pl.semaphore_signal(barrier, inc=1, device_id=(up, b), device_id_type=MESH)
+
+    @pl.when(has_down)
+    def _():
+        pl.semaphore_signal(barrier, inc=1, device_id=(down, b), device_id_type=MESH)
+
     for d in range(1, lons):
         pl.semaphore_signal(barrier, inc=1, device_id=(j, lax.rem(b + d, lons)), device_id_type=MESH)
 
     load_x = pltpu.make_async_copy(x_ref.at[0], xv, load_sem.at[0])
     load_w = pltpu.make_async_copy(winds_ref, wv, load_sem.at[1])
     load_d = pltpu.make_async_copy(diff_ref, dv, load_sem.at[2])
+    load_c = pltpu.make_async_copy(cutoff_ref, cut_ref, load_sem.at[3])
     load_x.start()
+    load_c.start()
     load_w.start()
     load_d.start()
 
@@ -66,35 +75,20 @@
         e1[r + OFF] = zero_e
         e1[-r + OFF] = zero_e
 
+    for there, received in ((has_down, (l1, l2, l3)), (has_up, (r1, r2, r3))):
+        @pl.when(jnp.logical_not(there))
+        def _():
+            @pl.loop(OFF - 18, OFF + 19)
+            def _(n):
+                for ref in received:
+                    ref[n] = zero
+
+    load_c.wait()
     load_x.wait()
 
     @pl.loop(OFF - WIDE, OFF + WIDE + 1)
     def _(n):
         xm[n] = xv[lat_of(n)] * keep(n)
-
-    pl.semaphore_wait(barrier, 2 + lons - 1)
-
-    def exchange(level, bounds, index, source, from_down, from_up, low, high):
-        a, e = pieces(bounds, low, high)[index]
-        to_up = pltpu.make_async_remote_copy(
-            source.at[pl.ds(a + 1 + OFF, e - a)], from_down.at[pl.ds(a + OFF, e - a)],
-            s_send.at[level, 0, index], s_recv.at[level, 0, index], device_id=(up, b), device_id_type=MESH)
-        a, e = pieces(bounds, -high, -low)[index]
-        to_down = pltpu.make_async_remote_copy(
-            source.at[pl.ds(a - 1 + OFF, e - a)], from_up.at[pl.ds(a + OFF, e - a)],
-            s_send.at[level, 1, index], s_recv.at[level, 1, index], device_id=(down, b), device_id_type=MESH)
-        return to_up, to_down
-
-    level1 = [exchange(0, B1, n, xm, l1, r1, -17, 15) for n in range(len(B1) - 1)]
-    level2 = [exchange(1, B2, n, h1, l2, r2, -17, 17) for n in range(len(B2) - 1)]
-    level3 = [exchange(2, B3, n, h2, l3, r3, -16, 16) for n in range(len(B3) - 1)]
-
-    def begin(copies):
-        for copy in copies:
-            copy.start()
-
-    for copies in level1:
-        begin(copies)
 
     load_w.wait()
     load_d.wait()
@@ -112,13 +106,49 @@
         mine.append(jnp.sum(table[:, OFF:OFF + 1] * place, axis=0, keepdims=True))
     mine.append(jnp.zeros((1, 128), jnp.float32))
     gath[b] = jnp.concatenate(mine, axis=0)
-    gathers = []
-    for d in range(1, lons):
-        copy = pltpu.make_async_remote_copy(
-            gath.at[b], gath.at[b], g_send.at[d - 1], g_recv.at[d - 1],
-            device_id=(j, lax.rem(b + d, lons)), device_id_type=MESH)
-        copy.start()
-        gathers.append(copy)
+
+    inner = jnp.logical_and(has_up, has_down)
+
+    @pl.when(inner)
+    def _():
+        pl.semaphore_wait(barrier, lons + 1)
+
+    @pl.when(jnp.logical_not(inner))
+    def _():
+        pl.semaphore_wait(barrier, lons)
+
+    def exchange(level, bounds, index, source, from_down, from_up, low, high):
+        a, e = pieces(bounds, low, high)[index]
+        to_up = pltpu.make_async_remote_copy(
+            source.at[pl.ds(a + 1 + OFF, e - a)], from_down.at[pl.ds(a + OFF, e - a)],
+            s_send.at[level, 0, index], s_recv.at[level, 0, index], device_id=(up, b), device_id_type=MESH)
+        a, e = pieces(bounds, -high, -low)[index]
+        to_down = pltpu.make_async_remote_copy(
+            source.at[pl.ds(a - 1 + OFF, e - a)], from_up.at[pl.ds(a + OFF, e - a)],
+            s_send.at[level, 1, index], s_recv.at[level, 1, index], device_id=(down, b), device_id_type=MESH)
+        return to_up, to_down
+
+    level1 = [exchange(0, B1, n, xm, l1, r1, -17, 15) for n in range(len(B1) - 1)]
+    level2 = [exchange(1, B2, n, h1, l2, r2, -17, 17) for n in range(len(B2) - 1)]
+    level3 = [exchange(2, B3, n, h2, l3, r3, -16, 16) for n in range(len(B3) - 1)]
+
+    def begin(copies):
+        for copy in copies:
+            copy.start()
+
+    def send(pair):
+        for there, copy in zip((has_up, has_down), pair):
+            @pl.when(there)
+            def _():
+                copy.start()
+
+    def receive(pair):
+        for there, copy in zip((has_down, has_up), pair):
+            @pl.when(there)
+            def _():
+                copy.wait_recv()
+
+    send(level1[0])
 
     lo, hi = pl.ds(0, HALO), pl.ds(HALO + 16, HALO)
     first, last = pl.ds(HALO, HALO), pl.ds(16, HALO)
@@ -135,6 +165,15 @@
 
     tables = halo(tab, t_send, t_recv)
     begin(tables)
+    gathers = []
+    for d in range(1, lons):
+        copy = pltpu.make_async_remote_copy(
+            gath.at[b], gath.at[b], g_send.at[d - 1], g_recv.at[d - 1],
+            device_id=(j, lax.rem(b + d, lons)), device_id_type=MESH)
+        copy.start()
+        gathers.append(copy)
+    send(level1[1])
+    send(level1[2])
 
     @pl.loop(OFF + WIDE + 1, OFF + NLAT - WIDE)
     def _(n):
@@ -146,15 +185,12 @@
     for d in range(1, lons):
         whole = whole + gath[d]
     k = whole[6:7]
-    open_down = jnp.where(j == 0, 0.0, 1.0).astype(jnp.float32)
-    open_up = jnp.where(j == NLAT - 1, 0.0, 1.0).astype(jnp.float32)
 
     def second(step, center, lower, upper):
         u, v = whole[step:step + 1], whole[3 + step:4 + step]
         c_w, c_e = k + jnp.maximum(u, 0.0), k - jnp.minimum(u, 0.0)
         c_s, c_n = k + jnp.maximum(v, 0.0), k - jnp.minimum(v, 0.0)
         c_0 = 1.0 - (c_w + c_e) - (c_s + c_n)
-        c_s, c_n = c_s * open_down, c_n * open_up
         return (c_0 * center + c_w * pltpu.roll(center, 1, 1) + c_e * pltpu.roll(center, 127, 1)
                 + c_s * lower + c_n * upper)
 
@@ -165,8 +201,9 @@
         lax.fori_loop(a + OFF, e + OFF, run, 0)
 
     def do_g1(index):
-        for copy in level1[index]:
-            copy.wait_recv()
+        receive(level1[index])
+        if index + 3 < len(level1):
+            send(level1[index + 3])
         a, e = B1[index], B1[index + 1]
 
         def body(n):
@@ -218,16 +255,14 @@
             done[step] = stop
 
     def do_h2(index):
-        for copy in level2[index]:
-            copy.wait_recv()
+        receive(level2[index])
 
         def body(n):
             h2[n] = second(1, h1[n], l2[n], r2[n])
         loop(B2[index], B2[index + 1], body)
 
     def do_out(index):
-        for copy in level3[index]:
-            copy.wait_recv()
+        receive(level3[index])
 
         def body(n):
             out_ref[0, lat_of(n)] = second(2, h2[n], l3[n], r3[n]) * keep(n)
@@ -246,7 +281,7 @@
 
     def a1_for(index):
         do_a1(B2[index + 1] + 1)
-        begin(level2[index])
+        send(level2[index])
 
     wait_halo(0)
     a1_for(0)
@@ -264,11 +299,16 @@
     a1_for(5)
     for n in range(len(B2) - 1):
         do_h2(n)
-        begin(level3[n])
+        send(level3[n])
     for n in range(len(B3) - 1):
         do_out(n)
 
-    for copies in level1 + level2 + level3 + halos + [tables] + [gathers]:
+    for pair in level1 + level2 + level3:
+        for there, copy in zip((has_up, has_down), pair):
+            @pl.when(there)
+            def _():
+                copy.wait_send()
+    for copies in halos + [tables] + [gathers]:
         for copy in copies:
             copy.wait_send()
 
@@ -283,20 +323,21 @@
     return pl.pallas_call(
         functools.partial(kernel, lats, lons),
         out_shape=jax.ShapeDtypeStruct(covariance.shape, jnp.float32),
-        in_specs=[pl.BlockSpec(memory_space=pl.ANY)] * 3 + [pl.BlockSpec(memory_space=pltpu.SMEM)],
+        in_specs=[pl.BlockSpec(memory_space=pltpu.HBM)] * 4,
         out_specs=pl.BlockSpec(memory_space=pltpu.VMEM),
         scratch_shapes=[
-            vm(NLAT, 16, 128), vm(*block), vm(2, 3, 16, NLAT), vm(16, NLAT),
+            pltpu.SMEM((NLAT,), jnp.int32), vm(NLAT, 16, 128), vm(*block), vm(2, 3, 16, NLAT), vm(16, NLAT),
             vm(*block), vm(*block), vm(*block), vm(*block), vm(*block), vm(*block),
             vm(*ext), vm(*ext), vm(*ext), vm(*block), vm(*block),
             vm(3, 5, *ext), vm(7, 16 + 2 * HALO, 128), vm(lons, 8, 128),
-            dma(3), dma(3, 2, most), dma(3, 2, most), dma(len(B1) - 1, 2), dma(len(B1) - 1, 2),
+            dma(4), dma(3, 2, most), dma(3, 2, most), dma(len(B1) - 1, 2), dma(len(B1) - 1, 2),
             dma(2), dma(2), dma(lons - 1), dma(lons - 1),
         ],
         compiler_params=pltpu.CompilerParams(
             collective_id=0, has_side_effects=True, vmem_limit_bytes=40 * 1024 * 1024),
         cost_estimate=pl.CostEstimate(flops=20_000_000, bytes_accessed=1_500_000, transcendentals=0),
-    )(covariance, jnp.transpose(winds, (0, 1, 3, 2)), jnp.transpose(diffusivity), cutoff)
+    )(*(pltpu.with_memory_space_constraint(a, pltpu.HBM) for a in (
+        covariance, jnp.transpose(winds, (0, 1, 3, 2)), jnp.transpose(diffusivity), cutoff)))
 
 
 def solution(mesh):

time: 46.4 us -> 39 us (0.84)
  the two profiles are of different devices: /device:TPU:1 before, /device:TPU:24 now
where the time goes in v2:
time: 39 us; the launch traced here: 38.8 us
  Pallas kernels  38 us (97%)
  local copies, waits for them, and re-layouts  0.8 us (2%)
    pallas_call x1, Pallas kernels, per_device(): pl.pallas_call(functools.partial(kernel, lats, lons), out_shape=jax.Shape...  38 us
    unnamed x1, local copies, waits for them, and re-layouts  0.8 us

profile of v2, /device:TPU:24, one launch (start us, length us, event | category | flops | bytes accessed | tf_op | source)
XLA Modules:
  0.0 38.8 jit_solution(3771429251872505875)
XLA Ops:
  0.0 38.0 %shard_map.46 = f32[1,64,16,128]{3,2,1,0:T(8,128)S(1)} custom-call(f32[1,64,16,128]{3,2,1,0:T(8,128)} %x_ref.1, f32[2,3,16,64]{3,2,1,0:T(8,128)} %bitcast.2, f32[16,64]{1,0:T(8,128)} %bitcast.3, s32[64]{0:T(128)} %cutoff_ref.1), custom_call_target="tpu_custom_call" | custom-call | flops 20000000 | bytes 1500000 | tf_op jit(solution)/shard_map/pallas_call | solution.py:323
  38.0 0.8 %copy.6 = f32[1,64,16,128]{3,2,1,0:T(8,128)} copy(f32[1,64,16,128]{3,2,1,0:T(8,128)S(1)} %shard_map.46) | data formatting | bytes 1048576

commit v3 on v2

v3 whole, which is shorter than its diff:
```python
import functools

import jax
import jax.numpy as jnp
from jax import lax
from jax.experimental import pallas as pl
from jax.experimental.pallas import tpu as pltpu
from jax.sharding import PartitionSpec as P

MESH = pl.DeviceIdType.MESH
NLAT = 64
WIDE = 16
REACH = 3
OFF = 22
ROWS = 2 * OFF + 1
HALO = 8
BOUNDS = (-19, -10, -1, 8, 14, 20)
PIECES = len(BOUNDS) - 1
NEEDED = ([(f, t) for f in (0, 3, 6) for t in range(-2, 3)] + [(f, t) for f in (1, 4) for t in range(-1, 2)]
          + [(2, 0), (5, 0)])
PACKED = 24


def piece(index, sign):
    low = max(BOUNDS[index] + sign * REACH, -WIDE)
    high = min(BOUNDS[index + 1] + sign * REACH, WIDE + 1)
    return (low, high) if high > low else None


def kernel(lats, lons, x_ref, winds_ref, diff_ref, cutoff_ref, out_ref,
           cut_ref, xv, xm, wv, dv, l1, r1, l2, r2, l3, r3, e0, e1, e2, co, tab, gath, taps,
           load_sem, s_send, s_recv, p_send, p_recv, t_send, t_recv, g_send, g_recv):
    j = lax.axis_index("lat")
    b = lax.axis_index("lon")
    up, down = lax.rem(j + 1, lats), lax.rem(j + lats - 1, lats)
    east, west = lax.rem(b + 1, lons), lax.rem(b + lons - 1, lons)
    has_up, has_down = j < lats - 1, j > 0

    barrier = pltpu.get_barrier_semaphore()

    @pl.when(has_up)
    def _():
        pl.semaphore_signal(barrier, inc=1, device_id=(up, b), device_id_type=MESH)

    @pl.when(has_down)
    def _():
        pl.semaphore_signal(barrier, inc=1, device_id=(down, b), device_id_type=MESH)

    for d in range(1, lons):
        pl.semaphore_signal(barrier, inc=1, device_id=(j, lax.rem(b + d, lons)), device_id_type=MESH)

    load_x = pltpu.make_async_copy(x_ref.at[0], xv, load_sem.at[0])
    load_w = pltpu.make_async_copy(winds_ref, wv, load_sem.at[1])
    load_d = pltpu.make_async_copy(diff_ref, dv, load_sem.at[2])
    load_c = pltpu.make_async_copy(cutoff_ref, cut_ref, load_sem.at[3])
    load_x.start()
    load_c.start()
    load_w.start()
    load_d.start()

    def lat_of(n):
        return lax.rem(j + n + (NLAT - OFF), NLAT)

    def keep(n):
        cut = cut_ref[lat_of(n)]
        inside = jnp.logical_and(j + n >= OFF, j + n < NLAT + OFF)
        near = jnp.logical_and(n <= OFF + cut, n + cut >= OFF)
        return jnp.where(jnp.logical_and(inside, near), 1.0, 0.0).astype(jnp.float32)

    zero = jnp.zeros((16, 128), jnp.float32)
    wide_shape = (2 * HALO + 16, 128)

    load_c.wait()
    load_x.wait()

    @pl.loop(OFF - WIDE, OFF + WIDE + 1)
    def _(n):
        xm[n] = xv[lat_of(n)] * keep(n)

    load_w.wait()
    load_d.wait()
    fields = [wv.at[c, s] for c in range(2) for s in range(3)] + [dv]
    lane = lax.broadcasted_iota(jnp.int32, (NLAT, 128), 1)
    sub = lax.broadcasted_iota(jnp.int32, (NLAT, 128), 0)
    turn = jnp.where(lane == sub - j + OFF, 1.0, 0.0).astype(jnp.float32)
    lane = lax.broadcasted_iota(jnp.int32, (16, 128), 1)
    sub = lax.broadcasted_iota(jnp.int32, (16, 128), 0)
    place = jnp.where(lane == sub + b * 16, 1.0, 0.0).astype(jnp.float32)
    tables_own = []
    for n, f in enumerate(fields):
        table = jnp.dot(f[...], turn, precision=lax.Precision.HIGHEST, preferred_element_type=jnp.float32)
        tab[n, HALO:HALO + 16, :] = table
        tables_own.append(table)
    mine = [jnp.sum(tables_own[f][:, OFF + t:OFF + t + 1] * place, axis=0, keepdims=True) for f, t in NEEDED]
    mine += [jnp.zeros((1, 128), jnp.float32)] * (PACKED - len(mine))
    gath[b] = jnp.concatenate(mine, axis=0)

    inner = jnp.logical_and(has_up, has_down)

    @pl.when(inner)
    def _():
        pl.semaphore_wait(barrier, lons + 1)

    @pl.when(jnp.logical_not(inner))
    def _():
        pl.semaphore_wait(barrier, lons)

    below, above = (xm, l1, l2, l3), (xm, r1, r2, r3)

    def hop(level, index, sign):
        rows = piece(index, sign)
        if rows is None:
            return None
        at = pl.ds(rows[0] + OFF, rows[1] - rows[0])
        held, way = (below, 0) if sign > 0 else (above, 1)
        return pltpu.make_async_remote_copy(
            held[level].at[at], held[level + 1].at[at], s_send.at[level, way, index], s_recv.at[level, way, index],
            device_id=(up if sign > 0 else down, b), device_id_type=MESH)

    hops = [[(hop(level, n, 1), hop(level, n, -1)) for n in range(PIECES)] for level in range(REACH)]

    def on_pair(pair, conditions, act):
        for there, copy in zip(conditions, pair):
            if copy is not None:
                @pl.when(there)
                def _():
                    act(copy)

    def sends(level):
        return (jnp.logical_and(has_up, j >= level), jnp.logical_and(has_down, j < lats - level))

    def send(level, index):
        on_pair(hops[level][index], sends(level), lambda copy: copy.start())

    def receive(level, index):
        on_pair(hops[level][index], (j > level, j < lats - 1 - level), lambda copy: copy.wait_recv())

    lo, hi = pl.ds(0, HALO), pl.ds(HALO + 16, HALO)
    first, last = pl.ds(HALO, HALO), pl.ds(16, HALO)

    def halo(ref, send_sem, recv_sem, rows=None):
        rows = slice(None) if rows is None else rows
        to_east = pltpu.make_async_remote_copy(
            ref.at[rows, last], ref.at[rows, lo], send_sem.at[0], recv_sem.at[0],
            device_id=(j, east), device_id_type=MESH)
        to_west = pltpu.make_async_remote_copy(
            ref.at[rows, first], ref.at[rows, hi], send_sem.at[1], recv_sem.at[1],
            device_id=(j, west), device_id_type=MESH)
        return to_east, to_west

    send(0, 0)
    send(0, 1)
    tables = halo(tab, t_send, t_recv)
    for copy in tables:
        copy.start()
    gathers = []
    for d in range(1, lons):
        copy = pltpu.make_async_remote_copy(
            gath.at[b], gath.at[b], g_send.at[d - 1], g_recv.at[d - 1],
            device_id=(j, lax.rem(b + d, lons)), device_id_type=MESH)
        copy.start()
        gathers.append(copy)
    for n in range(2, PIECES):
        send(0, n)

    for r in range(WIDE + 1, OFF + 1):
        for ref in (xm, l1, r1, l2, r2, l3, r3):
            ref[r + OFF] = zero
            ref[-r + OFF] = zero
    for level in range(REACH):
        for there, ref in ((j > level, below[level + 1]), (j < lats - 1 - level, above[level + 1])):
            @pl.when(jnp.logical_not(there))
            def _():
                @pl.loop(OFF - WIDE, OFF + WIDE + 1)
                def _(n):
                    ref[n] = zero

    @pl.loop(OFF + WIDE + 1, OFF + NLAT - WIDE)
    def _(n):
        out_ref[0, lat_of(n)] = zero

    for copy in gathers:
        copy.wait_recv()
    whole = gath[0]
    for d in range(1, lons):
        whole = whole + gath[d]
    known = {at: whole[n:n + 1] for n, at in enumerate(NEEDED)}

    def turned(value, d):
        return pltpu.roll(value, (-d) % 128, 1) if d else value

    def stencil(step, t):
        u, v, k = known[step, t], known[3 + step, t], known[6, t]
        c_w, c_e = k + jnp.maximum(u, 0.0), k - jnp.minimum(u, 0.0)
        c_s, c_n = k + jnp.maximum(v, 0.0), k - jnp.minimum(v, 0.0)
        return {(0, 0): 1.0 - (c_w + c_e) - (c_s + c_n), (0, -1): c_w, (0, 1): c_e, (-1, 0): c_s, (1, 0): c_n}

    composed = stencil(2, 0)
    for step in (1, 0):
        parts = {}
        for (t, d), weight in composed.items():
            for (dt, dd), value in stencil(step, t).items():
                parts.setdefault((t + dt, d + dd), []).append(weight * turned(value, d))
        composed = {at: functools.reduce(jnp.add, terms) for at, terms in parts.items()}
    slots = {at: n for n, at in enumerate(sorted(composed))}
    for at, n in slots.items():
        taps[n] = jnp.broadcast_to(composed[at], (8, 128))

    def add_rows(a, e, sources, fresh):
        weights = [(t, d, jnp.concatenate([taps[n]] * 2, axis=0)) for (t, d), n in slots.items() if t in sources]

        def run(n, carry):
            total = None if fresh else e0[n, HALO:HALO + 16, :]
            for t in sources:
                center = sources[t][n - t]
                for at, d, weight in weights:
                    if at == t:
                        term = weight * turned(center, d)
                        total = term if total is None else total + term
            e0[n, HALO:HALO + 16, :] = total
            return carry
        lax.fori_loop(a + OFF, e + OFF, run, 0)

    def coefficients(a, e):
        for r in range(a, e):
            at = slice(r + OFF, r + OFF + 1)
            k_r = jnp.broadcast_to(tab[6, :, at], wide_shape)
            for s in range(3):
                u = jnp.broadcast_to(tab[s, :, at], wide_shape)
                v = jnp.broadcast_to(tab[3 + s, :, at], wide_shape)
                c_w, c_e = k_r + jnp.maximum(u, 0.0), k_r - jnp.minimum(u, 0.0)
                c_s, c_n = k_r + jnp.maximum(v, 0.0), k_r - jnp.minimum(v, 0.0)
                co[s, 0, r + OFF] = 1.0 - (c_w + c_e) - (c_s + c_n)
                co[s, 1, r + OFF] = c_w
                co[s, 2, r + OFF] = c_e
                co[s, 3, r + OFF] = c_s
                co[s, 4, r + OFF] = c_n

    def first_step(step, source, store, a, e):
        def run(n, carry):
            center = source[n]
            store(n, co[step, 0, n] * center + co[step, 1, n] * pltpu.roll(center, 1, 0)
                  + co[step, 2, n] * pltpu.roll(center, 2 * HALO + 15, 0)
                  + co[step, 3, n] * source[n - 1] + co[step, 4, n] * source[n + 1])
            return carry
        lax.fori_loop(a + OFF, e + OFF, run, 0)

    def store_1(n, value):
        e1[n] = value

    def store_2(n, value):
        e2[n] = value

    def store_3(n, value):
        out_ref[0, lat_of(n)] = value[HALO:HALO + 16] * keep(n)

    halos = [halo(e0, p_send.at[n], p_recv.at[n], pl.ds(BOUNDS[n] + OFF, BOUNDS[n + 1] - BOUNDS[n]))
             for n in range(PIECES)]
    done = [-18, -17, -16]

    def finish(index):
        for copy in halos[index]:
            copy.wait_recv()
        for step, (source, store) in enumerate(((e0, store_1), (e1, store_2), (e2, store_3))):
            stop = BOUNDS[index + 1] - 1 - step
            first_step(step, source, store, done[step], stop)
            done[step] = stop

    for n in range(PIECES):
        receive(0, n)
        send(1, n)
        if n == 0:
            for copy in tables:
                copy.wait_recv()
            coefficients(-18, -6)
        if n == 1:
            coefficients(-6, 6)
        if n == 2:
            coefficients(6, 19)
    add_rows(-19, 20, {-1: l1, 0: xm, 1: r1}, True)
    for n in range(PIECES):
        receive(1, n)
        send(2, n)
        add_rows(BOUNDS[n] + (1 if n else 0), BOUNDS[n + 1] + (1 if n < PIECES - 1 else 0), {-2: l2}, False)
        add_rows(BOUNDS[n] - (1 if n else 0), BOUNDS[n + 1] - (1 if n < PIECES - 1 else 0), {2: r2}, False)
    for n in range(PIECES):
        receive(2, n)
        add_rows(BOUNDS[n], BOUNDS[n + 1], {-3: l3, 3: r3}, False)
        for copy in halos[n]:
            copy.start()
        if n >= 2:
            finish(n - 2)
    finish(PIECES - 2)
    finish(PIECES - 1)

    for level in range(REACH):
        for n in range(PIECES):
            on_pair(hops[level][n], sends(level), lambda copy: copy.wait_send())
    for copies in halos + [tables] + [gathers]:
        for copy in copies:
            copy.wait_send()


def per_device(covariance, winds, diffusivity, cutoff):
    lats, lons = lax.axis_size("lat"), lax.axis_size("lon")
    vm = lambda *shape: pltpu.VMEM(shape, jnp.float32)
    dma = lambda *shape: pltpu.SemaphoreType.DMA(shape)
    block = (ROWS, 16, 128)
    ext = (ROWS, 16 + 2 * HALO, 128)
    return pl.pallas_call(
        functools.partial(kernel, lats, lons),
        out_shape=jax.ShapeDtypeStruct(covariance.shape, jnp.float32),
        in_specs=[pl.BlockSpec(memory_space=pltpu.HBM)] * 4,
        out_specs=pl.BlockSpec(memory_space=pltpu.VMEM),
        scratch_shapes=[
            pltpu.SMEM((NLAT,), jnp.int32), vm(NLAT, 16, 128), vm(*block), vm(2, 3, 16, NLAT), vm(16, NLAT),
            vm(*block), vm(*block), vm(*block), vm(*block), vm(*block), vm(*block),
            vm(*ext), vm(*ext), vm(*ext), vm(3, 5, *ext), vm(7, 16 + 2 * HALO, 128), vm(lons, PACKED, 128),
            vm(25, 8, 128),
            dma(4), dma(REACH, 2, PIECES), dma(REACH, 2, PIECES), dma(PIECES, 2), dma(PIECES, 2),
            dma(2), dma(2), dma(lons - 1), dma(lons - 1),
        ],
        compiler_params=pltpu.CompilerParams(
            collective_id=0, has_side_effects=True, vmem_limit_bytes=40 * 1024 * 1024),
        cost_estimate=pl.CostEstimate(flops=20_000_000, bytes_accessed=1_500_000, transcendentals=0),
    )(*(pltpu.with_memory_space_constraint(a, pltpu.HBM) for a in (
        covariance, jnp.transpose(winds, (0, 1, 3, 2)), jnp.transpose(diffusivity), cutoff)))


def solution(mesh):
    in_specs = (P("lat", None, "lon", None), P(None, None, None, "lon"), P(None, "lon"), P())
    out_specs = P("lat", None, "lon", None)
    return jax.shard_map(
        per_device, mesh=mesh, in_specs=in_specs, out_specs=out_specs, check_vma=False
    )
```

time: 39 us -> 39.5 us (1.013)
  Pallas kernels: 38 us -> 38.6 us
    pallas_call x1, Pallas kernels: 38 us -> 38.6 us  [per_device(): pl.pallas_call(functools.partial(kernel, lats, lons), out_shape=jax.Shape...]
where the time goes in v3:
time: 39.5 us; the launch traced here: 39.4 us
  Pallas kernels  38.6 us (98%)
  local copies, waits for them, and re-layouts  0.8 us (2%)
    pallas_call x1, Pallas kernels, per_device(): pl.pallas_call(functools.partial(kernel, lats, lons), out_shape=jax.Shape...  38.6 us
    unnamed x1, local copies, waits for them, and re-layouts  0.8 us

profile of v3, /device:TPU:24, one launch (start us, length us, event | category | flops | bytes accessed | tf_op | source)
XLA Modules:
  0.0 39.4 jit_solution(6517911674494310622)
XLA Ops:
  0.0 38.6 %shard_map.46 = f32[1,64,16,128]{3,2,1,0:T(8,128)S(1)} custom-call(f32[1,64,16,128]{3,2,1,0:T(8,128)} %x_ref.1, f32[2,3,16,64]{3,2,1,0:T(8,128)} %bitcast.2, f32[16,64]{1,0:T(8,128)} %bitcast.3, s32[64]{0:T(128)} %cutoff_ref.1), custom_call_target="tpu_custom_call" | custom-call | flops 20000000 | bytes 1500000 | tf_op jit(solution)/shard_map/pallas_call | solution.py:310
  38.6 0.8 %copy.6 = f32[1,64,16,128]{3,2,1,0:T(8,128)} copy(f32[1,64,16,128]{3,2,1,0:T(8,128)S(1)} %shard_map.46) | data formatting | bytes 1048576

commit v4 on v3

--- a/solution.py
+++ b/solution.py
@@ -14,7 +14,8 @@
 OFF = 22
 ROWS = 2 * OFF + 1
 HALO = 8
-BOUNDS = (-19, -10, -1, 8, 14, 20)
+GROUP = 3
+BOUNDS = (-19, -4, 11, 20)
 PIECES = len(BOUNDS) - 1
 NEEDED = ([(f, t) for f in (0, 3, 6) for t in range(-2, 3)] + [(f, t) for f in (1, 4) for t in range(-1, 2)]
           + [(2, 0), (5, 0)])
@@ -76,6 +77,62 @@
     @pl.loop(OFF - WIDE, OFF + WIDE + 1)
     def _(n):
         xm[n] = xv[lat_of(n)] * keep(n)
+
+    inner = jnp.logical_and(has_up, has_down)
+
+    @pl.when(inner)
+    def _():
+        pl.semaphore_wait(barrier, lons + 1)
+
+    @pl.when(jnp.logical_not(inner))
+    def _():
+        pl.semaphore_wait(barrier, lons)
+
+    below, above = (xm, l1, l2, l3), (xm, r1, r2, r3)
+
+    def hop(level, index, sign):
+        rows = piece(index, sign)
+        if rows is None:
+            return None
+        at = pl.ds(rows[0] + OFF, rows[1] - rows[0])
+        held, way = (below, 0) if sign > 0 else (above, 1)
+        return pltpu.make_async_remote_copy(
+            held[level].at[at], held[level + 1].at[at], s_send.at[level, way, index], s_recv.at[level, way, index],
+            device_id=(up if sign > 0 else down, b), device_id_type=MESH)
+
+    hops = [[(hop(level, n, 1), hop(level, n, -1)) for n in range(PIECES)] for level in range(REACH)]
+
+    def on_pair(pair, conditions, act):
+        for there, copy in zip(conditions, pair):
+            if copy is not None:
+                @pl.when(there)
+                def _():
+                    act(copy)
+
+    def sends(level):
+        return (jnp.logical_and(has_up, j >= level), jnp.logical_and(has_down, j < lats - level))
+
+    def send(level, index):
+        on_pair(hops[level][index], sends(level), lambda copy: copy.start())
+
+    def receive(level, index):
+        on_pair(hops[level][index], (j > level, j < lats - 1 - level), lambda copy: copy.wait_recv())
+
+    lo, hi = pl.ds(0, HALO), pl.ds(HALO + 16, HALO)
+    first, last = pl.ds(HALO, HALO), pl.ds(16, HALO)
+
+    def halo(ref, send_sem, recv_sem, rows=None):
+        rows = slice(None) if rows is None else rows
+        to_east = pltpu.make_async_remote_copy(
+            ref.at[rows, last], ref.at[rows, lo], send_sem.at[0], recv_sem.at[0],
+            device_id=(j, east), device_id_type=MESH)
+        to_west = pltpu.make_async_remote_copy(
+            ref.at[rows, first], ref.at[rows, hi], send_sem.at[1], recv_sem.at[1],
+            device_id=(j, west), device_id_type=MESH)
+        return to_east, to_west
+
+    for n in range(PIECES):
+        send(0, n)
 
     load_w.wait()
     load_d.wait()
@@ -95,61 +152,6 @@
     mine += [jnp.zeros((1, 128), jnp.float32)] * (PACKED - len(mine))
     gath[b] = jnp.concatenate(mine, axis=0)
 
-    inner = jnp.logical_and(has_up, has_down)
-
-    @pl.when(inner)
-    def _():
-        pl.semaphore_wait(barrier, lons + 1)
-
-    @pl.when(jnp.logical_not(inner))
-    def _():
-        pl.semaphore_wait(barrier, lons)
-
-    below, above = (xm, l1, l2, l3), (xm, r1, r2, r3)
-
-    def hop(level, index, sign):
-        rows = piece(index, sign)
-        if rows is None:
-            return None
-        at = pl.ds(rows[0] + OFF, rows[1] - rows[0])
-        held, way = (below, 0) if sign > 0 else (above, 1)
-        return pltpu.make_async_remote_copy(
-            held[level].at[at], held[level + 1].at[at], s_send.at[level, way, index], s_recv.at[level, way, index],
-            device_id=(up if sign > 0 else down, b), device_id_type=MESH)
-
-    hops = [[(hop(level, n, 1), hop(level, n, -1)) for n in range(PIECES)] for level in range(REACH)]
-
-    def on_pair(pair, conditions, act):
-        for there, copy in zip(conditions, pair):
-            if copy is not None:
-                @pl.when(there)
-                def _():
-                    act(copy)
-
-    def sends(level):
-        return (jnp.logical_and(has_up, j >= level), jnp.logical_and(has_down, j < lats - level))
-
-    def send(level, index):
-        on_pair(hops[level][index], sends(level), lambda copy: copy.start())
-
-    def receive(level, index):
-        on_pair(hops[level][index], (j > level, j < lats - 1 - level), lambda copy: copy.wait_recv())
-
-    lo, hi = pl.ds(0, HALO), pl.ds(HALO + 16, HALO)
-    first, last = pl.ds(HALO, HALO), pl.ds(16, HALO)
-
-    def halo(ref, send_sem, recv_sem, rows=None):
-        rows = slice(None) if rows is None else rows
-        to_east = pltpu.make_async_remote_copy(
-            ref.at[rows, last], ref.at[rows, lo], send_sem.at[0], recv_sem.at[0],
-            device_id=(j, east), device_id_type=MESH)
-        to_west = pltpu.make_async_remote_copy(
-            ref.at[rows, first], ref.at[rows, hi], send_sem.at[1], recv_sem.at[1],
-            device_id=(j, west), device_id_type=MESH)
-        return to_east, to_west
-
-    send(0, 0)
-    send(0, 1)
     tables = halo(tab, t_send, t_recv)
     for copy in tables:
         copy.start()
@@ -160,8 +162,6 @@
             device_id=(j, lax.rem(b + d, lons)), device_id_type=MESH)
         copy.start()
         gathers.append(copy)
-    for n in range(2, PIECES):
-        send(0, n)
 
     for r in range(WIDE + 1, OFF + 1):
         for ref in (xm, l1, r1, l2, r2, l3, r3):
@@ -187,7 +187,20 @@
     known = {at: whole[n:n + 1] for n, at in enumerate(NEEDED)}
 
     def turned(value, d):
-        return pltpu.roll(value, (-d) % 128, 1) if d else value
+        return pltpu.roll(value, (-d) % 128, value.ndim - 1) if d else value
+
+    def by_groups(a, e, body):
+        count = (e - a) // GROUP
+
+        def run(g, carry):
+            body(a + OFF + g * GROUP, GROUP)
+            return carry
+        if count > 1:
+            lax.fori_loop(0, count, run, 0)
+        elif count:
+            body(a + OFF, GROUP)
+        if e - a > count * GROUP:
+            body(a + OFF + count * GROUP, e - a - count * GROUP)
 
     def stencil(step, t):
         u, v, k = known[step, t], known[3 + step, t], known[6, t]
@@ -209,17 +222,17 @@
     def add_rows(a, e, sources, fresh):
         weights = [(t, d, jnp.concatenate([taps[n]] * 2, axis=0)) for (t, d), n in slots.items() if t in sources]
 
-        def run(n, carry):
-            total = None if fresh else e0[n, HALO:HALO + 16, :]
+        def body(n, count):
+            rows = pl.ds(n, count)
+            total = None if fresh else e0[rows, HALO:HALO + 16, :]
             for t in sources:
-                center = sources[t][n - t]
+                center = sources[t][pl.ds(n - t, count)]
                 for at, d, weight in weights:
                     if at == t:
                         term = weight * turned(center, d)
                         total = term if total is None else total + term
-            e0[n, HALO:HALO + 16, :] = total
-            return carry
-        lax.fori_loop(a + OFF, e + OFF, run, 0)
+            e0[rows, HALO:HALO + 16, :] = total
+        by_groups(a, e, body)
 
     def coefficients(a, e):
         for r in range(a, e):
@@ -237,22 +250,23 @@
                 co[s, 4, r + OFF] = c_n
 
     def first_step(step, source, store, a, e):
-        def run(n, carry):
-            center = source[n]
-            store(n, co[step, 0, n] * center + co[step, 1, n] * pltpu.roll(center, 1, 0)
-                  + co[step, 2, n] * pltpu.roll(center, 2 * HALO + 15, 0)
-                  + co[step, 3, n] * source[n - 1] + co[step, 4, n] * source[n + 1])
-            return carry
-        lax.fori_loop(a + OFF, e + OFF, run, 0)
-
-    def store_1(n, value):
-        e1[n] = value
-
-    def store_2(n, value):
-        e2[n] = value
-
-    def store_3(n, value):
-        out_ref[0, lat_of(n)] = value[HALO:HALO + 16] * keep(n)
+        def body(n, count):
+            rows = pl.ds(n, count)
+            center = source[rows]
+            store(n, count, co[step, 0, rows] * center + co[step, 1, rows] * pltpu.roll(center, 1, 1)
+                  + co[step, 2, rows] * pltpu.roll(center, 2 * HALO + 15, 1)
+                  + co[step, 3, rows] * source[pl.ds(n - 1, count)] + co[step, 4, rows] * source[pl.ds(n + 1, count)])
+        by_groups(a, e, body)
+
+    def store_1(n, count, value):
+        e1[pl.ds(n, count)] = value
+
+    def store_2(n, count, value):
+        e2[pl.ds(n, count)] = value
+
+    def store_3(n, count, value):
+        for i in range(count):
+            out_ref[0, lat_of(n + i)] = value[i, HALO:HALO + 16] * keep(n + i)
 
     halos = [halo(e0, p_send.at[n], p_recv.at[n], pl.ds(BOUNDS[n] + OFF, BOUNDS[n + 1] - BOUNDS[n]))
              for n in range(PIECES)]

time: 39.5 us -> 36.6 us (0.927)
  the two profiles are of different devices: /device:TPU:24 before, /device:TPU:25 now
where the time goes in v4:
time: 36.6 us; the launch traced here: 36.5 us
  Pallas kernels  35.7 us (98%)
  local copies, waits for them, and re-layouts  0.8 us (2%)
    pallas_call x1, Pallas kernels, per_device(): pl.pallas_call(functools.partial(kernel, lats, lons), out_shape=jax.Shape...  35.7 us
    unnamed x1, local copies, waits for them, and re-layouts  0.8 us

profile of v4, /device:TPU:25, one launch (start us, length us, event | category | flops | bytes accessed | tf_op | source)
XLA Modules:
  0.0 36.5 jit_solution(14261731987833784974)
XLA Ops:
  0.0 35.7 %shard_map.46 = f32[1,64,16,128]{3,2,1,0:T(8,128)S(1)} custom-call(f32[1,64,16,128]{3,2,1,0:T(8,128)} %x_ref.1, f32[2,3,16,64]{3,2,1,0:T(8,128)} %bitcast.2, f32[16,64]{1,0:T(8,128)} %bitcast.3, s32[64]{0:T(128)} %cutoff_ref.1), custom_call_target="tpu_custom_call" | custom-call | flops 20000000 | bytes 1500000 | tf_op jit(solution)/shard_map/pallas_call | solution.py:324
  35.7 0.8 %copy.6 = f32[1,64,16,128]{3,2,1,0:T(8,128)} copy(f32[1,64,16,128]{3,2,1,0:T(8,128)S(1)} %shard_map.46) | data formatting | bytes 1048576

commit v5 on v4

--- a/solution.py
+++ b/solution.py
@@ -14,7 +14,7 @@
 OFF = 22
 ROWS = 2 * OFF + 1
 HALO = 8
-GROUP = 3
+GROUP = 6
 BOUNDS = (-19, -4, 11, 20)
 PIECES = len(BOUNDS) - 1
 NEEDED = ([(f, t) for f in (0, 3, 6) for t in range(-2, 3)] + [(f, t) for f in (1, 4) for t in range(-1, 2)]
@@ -74,9 +74,11 @@
     load_c.wait()
     load_x.wait()
 
-    @pl.loop(OFF - WIDE, OFF + WIDE + 1)
-    def _(n):
-        xm[n] = xv[lat_of(n)] * keep(n)
+    @pl.loop(0, 11)
+    def _(g):
+        for i in range(3):
+            n = OFF - WIDE + 3 * g + i
+            xm[n] = xv[lat_of(n)] * keep(n)
 
     inner = jnp.logical_and(has_up, has_down)
 
@@ -117,6 +119,21 @@
 
     def receive(level, index):
         on_pair(hops[level][index], (j > level, j < lats - 1 - level), lambda copy: copy.wait_recv())
+
+    def forward(level, index):
+        for side in (0, 1):
+            come, go = hops[level][index][side], hops[level + 1][index][side]
+            if come is not None:
+                arrives = (j > level, j < lats - 1 - level)[side]
+                goes = sends(level + 1)[side]
+
+                @pl.when(arrives)
+                def _():
+                    come.wait_recv()
+
+                @pl.when(goes)
+                def _():
+                    go.start()
 
     lo, hi = pl.ds(0, HALO), pl.ds(HALO + 16, HALO)
     first, last = pl.ds(HALO, HALO), pl.ds(16, HALO)
@@ -281,8 +298,7 @@
             done[step] = stop
 
     for n in range(PIECES):
-        receive(0, n)
-        send(1, n)
+        forward(0, n)
         if n == 0:
             for copy in tables:
                 copy.wait_recv()
@@ -293,8 +309,7 @@
             coefficients(6, 19)
     add_rows(-19, 20, {-1: l1, 0: xm, 1: r1}, True)
     for n in range(PIECES):
-        receive(1, n)
-        send(2, n)
+        forward(1, n)
         add_rows(BOUNDS[n] + (1 if n else 0), BOUNDS[n + 1] + (1 if n < PIECES - 1 else 0), {-2: l2}, False)
         add_rows(BOUNDS[n] - (1 if n else 0), BOUNDS[n + 1] - (1 if n < PIECES - 1 else 0), {2: r2}, False)
     for n in range(PIECES):

time: 36.6 us -> 36.6 us (level)
  no operation moved by 1% of the time
where the time goes in v5:
time: 36.6 us; the launch traced here: 36.4 us
  Pallas kernels  35.6 us (97%)
  local copies, waits for them, and re-layouts  0.8 us (2%)
    pallas_call x1, Pallas kernels, per_device(): pl.pallas_call(functools.partial(kernel, lats, lons), out_shape=jax.Shape...  35.6 us
    unnamed x1, local copies, waits for them, and re-layouts  0.8 us

profile of v5, /device:TPU:25, one launch (start us, length us, event | category | flops | bytes accessed | tf_op | source)
XLA Modules:
  0.0 36.4 jit_solution(4190109196217910983)
XLA Ops:
  0.0 35.6 %shard_map.46 = f32[1,64,16,128]{3,2,1,0:T(8,128)S(1)} custom-call(f32[1,64,16,128]{3,2,1,0:T(8,128)} %x_ref.1, f32[2,3,16,64]{3,2,1,0:T(8,128)} %bitcast.2, f32[16,64]{1,0:T(8,128)} %bitcast.3, s32[64]{0:T(128)} %cutoff_ref.1), custom_call_target="tpu_custom_call" | custom-call | flops 20000000 | bytes 1500000 | tf_op jit(solution)/shard_map/pallas_call | solution.py:339
  35.6 0.8 %copy.6 = f32[1,64,16,128]{3,2,1,0:T(8,128)} copy(f32[1,64,16,128]{3,2,1,0:T(8,128)S(1)} %shard_map.46) | data formatting | bytes 1048576

commit v6 on v5

--- a/solution.py
+++ b/solution.py
@@ -15,7 +15,7 @@
 ROWS = 2 * OFF + 1
 HALO = 8
 GROUP = 6
-BOUNDS = (-19, -4, 11, 20)
+BOUNDS = (-19, -6, 9, 20)
 PIECES = len(BOUNDS) - 1
 NEEDED = ([(f, t) for f in (0, 3, 6) for t in range(-2, 3)] + [(f, t) for f in (1, 4) for t in range(-1, 2)]
           + [(2, 0), (5, 0)])
@@ -120,18 +120,18 @@
     def receive(level, index):
         on_pair(hops[level][index], (j > level, j < lats - 1 - level), lambda copy: copy.wait_recv())
 
-    def forward(level, index):
-        for side in (0, 1):
+    def forward(level, index, sides=(0, 1), when=True):
+        for side in sides:
             come, go = hops[level][index][side], hops[level + 1][index][side]
             if come is not None:
                 arrives = (j > level, j < lats - 1 - level)[side]
                 goes = sends(level + 1)[side]
 
-                @pl.when(arrives)
+                @pl.when(jnp.logical_and(arrives, when))
                 def _():
                     come.wait_recv()
 
-                @pl.when(goes)
+                @pl.when(jnp.logical_and(goes, when))
                 def _():
                     go.start()
 
@@ -308,8 +308,12 @@
         if n == 2:
             coefficients(6, 19)
     add_rows(-19, 20, {-1: l1, 0: xm, 1: r1}, True)
-    for n in range(PIECES):
-        forward(1, n)
+    early = lax.rem(j, 16) == 0
+    for n in range(PIECES):
+        forward(1, n, (1,), early)
+    for n in range(PIECES):
+        forward(1, n, (0,))
+        forward(1, n, (1,), jnp.logical_not(early))
         add_rows(BOUNDS[n] + (1 if n else 0), BOUNDS[n + 1] + (1 if n < PIECES - 1 else 0), {-2: l2}, False)
         add_rows(BOUNDS[n] - (1 if n else 0), BOUNDS[n + 1] - (1 if n < PIECES - 1 else 0), {2: r2}, False)
     for n in range(PIECES):

time: 36.6 us -> 36.5 us (level)
  no operation moved by 1% of the time
where the time goes in v6:
time: 36.5 us; the launch traced here: 36.4 us
  Pallas kernels  35.6 us (98%)
  local copies, waits for them, and re-layouts  0.8 us (2%)
    pallas_call x1, Pallas kernels, per_device(): pl.pallas_call(functools.partial(kernel, lats, lons), out_shape=jax.Shape...  35.6 us
    unnamed x1, local copies, waits for them, and re-layouts  0.8 us

profile of v6, /device:TPU:25, one launch (start us, length us, event | category | flops | bytes accessed | tf_op | source)
XLA Modules:
  0.0 36.4 jit_solution(15339892142702436282)
XLA Ops:
  0.0 35.6 %shard_map.46 = f32[1,64,16,128]{3,2,1,0:T(8,128)S(1)} custom-call(f32[1,64,16,128]{3,2,1,0:T(8,128)} %x_ref.1, f32[2,3,16,64]{3,2,1,0:T(8,128)} %bitcast.2, f32[16,64]{1,0:T(8,128)} %bitcast.3, s32[64]{0:T(128)} %cutoff_ref.1), custom_call_target="tpu_custom_call" | custom-call | flops 20000000 | bytes 1500000 | tf_op jit(solution)/shard_map/pallas_call | solution.py:343
  35.6 0.8 %copy.6 = f32[1,64,16,128]{3,2,1,0:T(8,128)} copy(f32[1,64,16,128]{3,2,1,0:T(8,128)S(1)} %shard_map.46) | data formatting | bytes 1048576
